TPU v7x, 32 devices: a whole 2x2x4 slice. The times are simulated.
32 devices in a mesh: blk: 8 (over y, x, core), lag: 4 (over z).
Axes of the slice: x: 2, y: 2, z: 4, core: 2. Of those that a mesh axis runs over, the one named last changes fastest.
Arguments:
- raw: float32 [8192, 4096], P(('blk', 'lag')), may hold values from -60 to 60
- mask: int32 [8, 8], replicated, may hold values from 0 to 1, as said below
Outputs:
- stack: float32 [8, 8192], P(None, ('blk', 'lag'))
Inputs may be any that keep to these rules, and one draw needn't show every extreme that they name: mask is 0 or 1 and symmetric; it is 0 wherever |I - J| exceeds a limit between 4 and 6.
All inputs are finite; a program needn't handle non-finite values.
Results may differ from a plain program's by a relative error of at most 0.008.
Values may be sent and summed in bfloat16 or wider, within the bound.
A program may use at most 192 MiB of HBM per device.

v0:
```python
import math

import jax
import jax.numpy as jnp
from jax import lax
from jax.sharding import PartitionSpec as P

NT = 8192
C = 4096
NB = 2048
K0 = 16
SW = 32
TAPER = 128
LAGS = 8
LAG_STEP = 32


EPS = 1e-06


def padded_2(x, sides, width):
    for axis, dim in sides:
        size, length = (lax.axis_size(axis), x.shape[dim])
        up = [(i, (i + 1) % size) for i in range(size - 1)]
        down = [(j, i) for i, j in up]
        last = lax.slice_in_dim(x, length - width, length, axis=dim)
        initial = lax.slice_in_dim(x, 0, width, axis=dim)
        before = lax.ppermute(last, axis, up)
        after = lax.ppermute(initial, axis, down)
        x = jnp.concatenate([before, x, after], axis=dim)
    return x


def from_behind(value, axis, steps):
    count = lax.axis_size(axis)
    pairs = [(source, (source + steps) % count) for source in range(count)]
    return lax.ppermute(value, axis, pairs)


def taper_weights(first_bin, count):
    position = (first_bin + lax.iota(jnp.int32, count)).astype(jnp.float32)
    edge = jnp.minimum(position, NB - 1 - position)
    curve = 0.5 - 0.5 * jnp.cos(math.pi * (edge + 0.5) / TAPER)
    return jnp.where(edge < TAPER, curve, jnp.ones_like(curve))


def lag_phases(bins):
    number = lax.iota(jnp.int32, LAGS)
    shifts = LAG_STEP * (2 * number + 1 - LAGS) // 2
    return jnp.mod(shifts[:, None] * bins[None, :], NT).astype(jnp.float32) * (2 * math.pi / NT)


def moving_mean(padded):
    window = lax.reduce_window(
        padded, jnp.zeros((), padded.dtype), lax.add, (1, 2 * SW + 1), (1, 1), "VALID"
    )
    return window / (2 * SW + 1)


def rotate(own_real, own_imag, cosines, sines):
    real_part = own_real.astype(jnp.float32)[None]
    imag_part = own_imag.astype(jnp.float32)[None]
    rot_real = real_part * cosines[:, None, :] - imag_part * sines[:, None, :]
    rot_imag = real_part * sines[:, None, :] + imag_part * cosines[:, None, :]
    joined = jnp.concatenate([rot_real, rot_imag], axis=2).astype(jnp.bfloat16)
    return joined.reshape(joined.shape[0] * joined.shape[1], joined.shape[2])


def diagonal_sums(product, rows):
    count = product.shape[2]
    padded = jnp.pad(product, ((0, 0), (0, 0), (0, rows)))
    width = count + rows - 1
    flat = padded.reshape(product.shape[0], rows * (count + rows))[:, : rows * width]
    return jnp.sum(flat.reshape(product.shape[0], rows, width), axis=1)


def place(total, values, first_col):
    anchor = jnp.zeros((), jnp.int32)
    current = lax.dynamic_slice(total, (anchor, first_col), values.shape)
    return lax.dynamic_update_slice(total, current + values, (anchor, first_col))


def pair_counts(mask, columns):
    blocks = mask.shape[0]
    width = C // blocks
    labels = lax.iota(jnp.int32, blocks)
    apart = labels[None, :] - labels[:, None]
    deltas = lax.iota(jnp.int32, 2 * blocks - 1) - (blocks - 1)
    per_delta = jnp.sum(
        mask[None] * (apart[None] == deltas[:, None, None]).astype(jnp.int32), axis=(1, 2)
    )
    offsets = columns - C
    intersection = jnp.maximum(0, width - jnp.abs(offsets[:, None] - width * deltas[None, :]))
    return jnp.sum(intersection * per_delta[None, :], axis=1)


def stack_scale(counts):
    return 1.0 / jnp.sqrt(NB * jnp.maximum(counts, 1).astype(jnp.float32))


def on_device(raw, mask):
    n_blk = lax.axis_size("blk")
    n_lag = lax.axis_size("lag")
    blk_id = lax.axis_index("blk")
    lag_id = lax.axis_index("lag")
    series = lax.all_to_all(
        raw.astype(jnp.bfloat16), ("blk", "lag"), split_axis=1, concat_axis=0, tiled=True
    ).astype(raw.dtype)
    own_chans = series.shape[1]
    band_bins = K0 + lax.iota(jnp.int32, NB)
    rows_blk = 1024
    offsets_in = lax.iota(jnp.int32, rows_blk)
    base_angle = jnp.mod(offsets_in[:, None] * band_bins[None, :], NT).astype(jnp.float32) * (
        2 * math.pi / NT
    )
    base_cos = jnp.cos(base_angle)
    base_sin = jnp.sin(base_angle)

    def transform_block(number, sums):
        start = number * rows_blk
        samples = lax.dynamic_slice_in_dim(series, start, rows_blk, 0)
        dims = (((0,), (0,)), ((), ()))
        part_cos = lax.dot_general(
            samples,
            base_cos,
            dims,
            precision=lax.Precision.HIGHEST,
            preferred_element_type=jnp.float32,
        )
        part_sin = lax.dot_general(
            samples,
            base_sin,
            dims,
            precision=lax.Precision.HIGHEST,
            preferred_element_type=jnp.float32,
        )
        shift_angle = jnp.mod(start * band_bins, NT).astype(jnp.float32) * (2 * math.pi / NT)
        shift_cos = jnp.cos(shift_angle)[None, :]
        shift_sin = jnp.sin(shift_angle)[None, :]
        real_add = part_cos * shift_cos - part_sin * shift_sin
        imag_add = part_sin * shift_cos + part_cos * shift_sin
        return (sums[0] + real_add, sums[1] - imag_add)

    empty = jnp.zeros((own_chans, NB), jnp.float32)
    real_spec, imag_spec = lax.fori_loop(0, NT // rows_blk, transform_block, (empty, empty))
    spectra = jnp.stack([real_spec, imag_spec], axis=1)
    banded = lax.all_to_all(
        spectra.astype(jnp.bfloat16), "lag", split_axis=2, concat_axis=0, tiled=True
    ).astype(spectra.dtype)
    rows = banded.shape[0]
    n_bins = banded.shape[2]
    real_band = banded[:, 0, :]
    imag_band = banded[:, 1, :]
    amplitude = jnp.sqrt(real_band * real_band + imag_band * imag_band)
    widened = padded_2(amplitude.astype(jnp.bfloat16), (("lag", 1),), SW).astype(amplitude.dtype)
    smooth = moving_mean(widened)
    first_bin = lag_id * n_bins
    weights = taper_weights(first_bin, n_bins)
    real_white = (real_band * weights[None, :] / (smooth + EPS)).astype(jnp.bfloat16)
    imag_white = (imag_band * weights[None, :] / (smooth + EPS)).astype(jnp.bfloat16)
    white = jnp.concatenate([real_white, imag_white], axis=1)
    phases = lag_phases(K0 + first_bin + lax.iota(jnp.int32, n_bins))
    rotated = rotate(real_white[::-1], imag_white[::-1], jnp.cos(phases), jnp.sin(phases))
    row_mask = lax.dynamic_index_in_dim(mask, blk_id, 0, keepdims=False)
    column_mask = jnp.repeat(row_mask, rows).astype(jnp.bfloat16)

    def contribution(piece, start):
        count = piece.shape[0]
        live = lax.dynamic_slice_in_dim(column_mask, start, count, 0)
        product = lax.dot_general(
            rotated,
            piece * live[:, None],
            (((1,), (1,)), ((), ())),
            preferred_element_type=jnp.float32,
        )
        diagonal = diagonal_sums(product.reshape(LAGS, rows, count), rows)
        first_col = start - blk_id * rows + C - rows + 1
        return (diagonal, first_col)

    initial = jnp.zeros((LAGS, 2 * C), jnp.float32)
    half = n_blk // 2
    diagonal, first_col = contribution(white, blk_id * rows)
    total = place(initial, diagonal, first_col)

    def mirror_block(number, state):
        total, block = state
        block = from_behind(block, "blk", -1)
        source = jnp.mod(blk_id + number, n_blk)
        diagonal, first_col = contribution(block, source * rows)
        keeper = jnp.where((number < half) | (blk_id < half), 1.0, 0.0).astype(jnp.float32)
        diagonal = diagonal * keeper
        width = diagonal.shape[1]
        total = place(total, diagonal, first_col)
        total = place(total, diagonal[::-1, ::-1], 2 * C - first_col - width + 1)
        return (total, block)

    total, _ = lax.fori_loop(1, half + 1, mirror_block, (total, white))
    shares = lax.psum_scatter(total, ("blk", "lag"), scatter_dimension=1, tiled=True)
    n_cols = shares.shape[1]
    device = blk_id * n_lag + lag_id
    columns = device * n_cols + lax.iota(jnp.int32, n_cols)
    counts = pair_counts(mask, columns)
    return shares * stack_scale(counts)[None, :]


def solution(mesh):
    return jax.shard_map(
        on_device,
        mesh=mesh,
        in_specs=(P(("blk", "lag"), None), P()),
        out_specs=P(None, ("blk", "lag")),
        check_vma=False,
    )
```

profile of v0, /device:TPU:0, one launch (start us, length us, event | category | flops | bytes accessed | tf_op | source)
XLA Modules:
  0.0 1450.5 jit_solution(14610573051295444316)
XLA Ops:
  17.9 47.5 %all-to-all-done = bf16[256,32,128]{2,0,1:T(8,128)(2,1)S(1)} async-done(((bf16[256,32,128]{2,0,1:T(8,128)(2,1)}), bf16[256,32,128]{2,0,1:T(8,128)(2,1)S(1)}, u32[]{:S(2)}, u32[]{:S(2)}) %all-to-all-start) | async-done | bytes 2097184 | tf_op jit(solution)/shard_map/all_to_all | solution.py:106
  67.8 645.7 %while.41 = (s32[]{:T(128)}, f32[128,2048]{1,0:T(8,128)S(1)}, f32[128,2048]{1,0:T(8,128)}, f32[8192,128]{1,0:T(8,128)}, s32[2048]{0:T(1024)S(1)}, /*index=5*/s32[]{:T(128)}, s32[]{:T(128)}, s32[]{:T(128)}, s32[]{:T(128)}) while((s32[]{:T(128)}, f32[128,2048]{1,0:T(8,128)S(1)}, f32[128,2048]{1,0:T(8,128)}, ...), condition=%wide.region_1.2_spmd.clone.clone.clone, body=%wide.region_0.1_spmd.clone.clone.clone.sunk | while | flops 6503823360 | bytes 15778009 | solution.py:145
  67.8 40.2 %fusion.61 = f32[128,2048]{1,0:T(8,128)} fusion(s32[2048]{0:T(1024)S(1)} %get-tuple-element.699, f32[8192,128]{1,0:T(8,128)} %get-tuple-element.698, s32[]{:T(128)S(6)} %select_n.244), kind=kOutput, calls=%fused_computation.15.clone.1 | convolution fusion | flops 3250585600 | bytes 1581060 | tf_op jit(solution)/shard_map/while/body/eval_jaxpr/dot_general | solution.py:130
  108.1 39.4 %select_subtract_fusion.2 = (f32[128,2048]{1,0:T(8,128)S(1)}, f32[128,2048]{1,0:T(8,128)S(1)}) fusion(f32[128,2048]{1,0:T(8,128)S(1)} %copy-done.5, f32[128,2048]{1,0:T(8,128)} %fusion.61, f32[2048]{0:T(1024)S(1)} %get-tuple-element.673, f32[2048]{0:T(1024)S(1)} %get-tuple-element.674, pred[]{:T(512)S(6)} %compare.28, ...), kind=kOutput, calls=%fused_computation.22.clone.1 | convolution fusion | flops 3253207040 | bytes 5791749 | tf_op jit(solution)/shard_map/while/body/eval_jaxpr/dot_general | solution.py:123
  148.5 40.2 %fusion.61 = f32[128,2048]{1,0:T(8,128)} fusion(s32[2048]{0:T(1024)S(1)} %get-tuple-element.699, f32[8192,128]{1,0:T(8,128)} %get-tuple-element.698, s32[]{:T(128)S(6)} %select_n.244), kind=kOutput, calls=%fused_computation.15.clone.1 | convolution fusion | flops 3250585600 | bytes 1581060 | tf_op jit(solution)/shard_map/while/body/eval_jaxpr/dot_general | solution.py:130
  188.8 39.4 %select_subtract_fusion.2 = (f32[128,2048]{1,0:T(8,128)S(1)}, f32[128,2048]{1,0:T(8,128)S(1)}) fusion(f32[128,2048]{1,0:T(8,128)S(1)} %copy-done.5, f32[128,2048]{1,0:T(8,128)} %fusion.61, f32[2048]{0:T(1024)S(1)} %get-tuple-element.673, f32[2048]{0:T(1024)S(1)} %get-tuple-element.674, pred[]{:T(512)S(6)} %compare.28, ...), kind=kOutput, calls=%fused_computation.22.clone.1 | convolution fusion | flops 3253207040 | bytes 5791749 | tf_op jit(solution)/shard_map/while/body/eval_jaxpr/dot_general | solution.py:123
  229.3 40.2 %fusion.61 = f32[128,2048]{1,0:T(8,128)} fusion(s32[2048]{0:T(1024)S(1)} %get-tuple-element.699, f32[8192,128]{1,0:T(8,128)} %get-tuple-element.698, s32[]{:T(128)S(6)} %select_n.244), kind=kOutput, calls=%fused_computation.15.clone.1 | convolution fusion | flops 3250585600 | bytes 1581060 | tf_op jit(solution)/shard_map/while/body/eval_jaxpr/dot_general | solution.py:130
  269.5 39.4 %select_subtract_fusion.2 = (f32[128,2048]{1,0:T(8,128)S(1)}, f32[128,2048]{1,0:T(8,128)S(1)}) fusion(f32[128,2048]{1,0:T(8,128)S(1)} %copy-done.5, f32[128,2048]{1,0:T(8,128)} %fusion.61, f32[2048]{0:T(1024)S(1)} %get-tuple-element.673, f32[2048]{0:T(1024)S(1)} %get-tuple-element.674, pred[]{:T(512)S(6)} %compare.28, ...), kind=kOutput, calls=%fused_computation.22.clone.1 | convolution fusion | flops 3253207040 | bytes 5791749 | tf_op jit(solution)/shard_map/while/body/eval_jaxpr/dot_general | solution.py:123
  310.0 40.2 %fusion.61 = f32[128,2048]{1,0:T(8,128)} fusion(s32[2048]{0:T(1024)S(1)} %get-tuple-element.699, f32[8192,128]{1,0:T(8,128)} %get-tuple-element.698, s32[]{:T(128)S(6)} %select_n.244), kind=kOutput, calls=%fused_computation.15.clone.1 | convolution fusion | flops 3250585600 | bytes 1581060 | tf_op jit(solution)/shard_map/while/body/eval_jaxpr/dot_general | solution.py:130
  350.2 39.4 %select_subtract_fusion.2 = (f32[128,2048]{1,0:T(8,128)S(1)}, f32[128,2048]{1,0:T(8,128)S(1)}) fusion(f32[128,2048]{1,0:T(8,128)S(1)} %copy-done.5, f32[128,2048]{1,0:T(8,128)} %fusion.61, f32[2048]{0:T(1024)S(1)} %get-tuple-element.673, f32[2048]{0:T(1024)S(1)} %get-tuple-element.674, pred[]{:T(512)S(6)} %compare.28, ...), kind=kOutput, calls=%fused_computation.22.clone.1 | convolution fusion | flops 3253207040 | bytes 5791749 | tf_op jit(solution)/shard_map/while/body/eval_jaxpr/dot_general | solution.py:123
  390.7 40.2 %fusion.61 = f32[128,2048]{1,0:T(8,128)} fusion(s32[2048]{0:T(1024)S(1)} %get-tuple-element.699, f32[8192,128]{1,0:T(8,128)} %get-tuple-element.698, s32[]{:T(128)S(6)} %select_n.244), kind=kOutput, calls=%fused_computation.15.clone.1 | convolution fusion | flops 3250585600 | bytes 1581060 | tf_op jit(solution)/shard_map/while/body/eval_jaxpr/dot_general | solution.py:130
  431.0 39.4 %select_subtract_fusion.2 = (f32[128,2048]{1,0:T(8,128)S(1)}, f32[128,2048]{1,0:T(8,128)S(1)}) fusion(f32[128,2048]{1,0:T(8,128)S(1)} %copy-done.5, f32[128,2048]{1,0:T(8,128)} %fusion.61, f32[2048]{0:T(1024)S(1)} %get-tuple-element.673, f32[2048]{0:T(1024)S(1)} %get-tuple-element.674, pred[]{:T(512)S(6)} %compare.28, ...), kind=kOutput, calls=%fused_computation.22.clone.1 | convolution fusion | flops 3253207040 | bytes 5791749 | tf_op jit(solution)/shard_map/while/body/eval_jaxpr/dot_general | solution.py:123
  471.4 40.2 %fusion.61 = f32[128,2048]{1,0:T(8,128)} fusion(s32[2048]{0:T(1024)S(1)} %get-tuple-element.699, f32[8192,128]{1,0:T(8,128)} %get-tuple-element.698, s32[]{:T(128)S(6)} %select_n.244), kind=kOutput, calls=%fused_computation.15.clone.1 | convolution fusion | flops 3250585600 | bytes 1581060 | tf_op jit(solution)/shard_map/while/body/eval_jaxpr/dot_general | solution.py:130
  511.7 39.4 %select_subtract_fusion.2 = (f32[128,2048]{1,0:T(8,128)S(1)}, f32[128,2048]{1,0:T(8,128)S(1)}) fusion(f32[128,2048]{1,0:T(8,128)S(1)} %copy-done.5, f32[128,2048]{1,0:T(8,128)} %fusion.61, f32[2048]{0:T(1024)S(1)} %get-tuple-element.673, f32[2048]{0:T(1024)S(1)} %get-tuple-element.674, pred[]{:T(512)S(6)} %compare.28, ...), kind=kOutput, calls=%fused_computation.22.clone.1 | convolution fusion | flops 3253207040 | bytes 5791749 | tf_op jit(solution)/shard_map/while/body/eval_jaxpr/dot_general | solution.py:123
  552.1 40.2 %fusion.61 = f32[128,2048]{1,0:T(8,128)} fusion(s32[2048]{0:T(1024)S(1)} %get-tuple-element.699, f32[8192,128]{1,0:T(8,128)} %get-tuple-element.698, s32[]{:T(128)S(6)} %select_n.244), kind=kOutput, calls=%fused_computation.15.clone.1 | convolution fusion | flops 3250585600 | bytes 1581060 | tf_op jit(solution)/shard_map/while/body/eval_jaxpr/dot_general | solution.py:130
  592.4 39.4 %select_subtract_fusion.2 = (f32[128,2048]{1,0:T(8,128)S(1)}, f32[128,2048]{1,0:T(8,128)S(1)}) fusion(f32[128,2048]{1,0:T(8,128)S(1)} %copy-done.5, f32[128,2048]{1,0:T(8,128)} %fusion.61, f32[2048]{0:T(1024)S(1)} %get-tuple-element.673, f32[2048]{0:T(1024)S(1)} %get-tuple-element.674, pred[]{:T(512)S(6)} %compare.28, ...), kind=kOutput, calls=%fused_computation.22.clone.1 | convolution fusion | flops 3253207040 | bytes 5791749 | tf_op jit(solution)/shard_map/while/body/eval_jaxpr/dot_general | solution.py:123
  632.8 40.2 %fusion.61 = f32[128,2048]{1,0:T(8,128)} fusion(s32[2048]{0:T(1024)S(1)} %get-tuple-element.699, f32[8192,128]{1,0:T(8,128)} %get-tuple-element.698, s32[]{:T(128)S(6)} %select_n.244), kind=kOutput, calls=%fused_computation.15.clone.1 | convolution fusion | flops 3250585600 | bytes 1581060 | tf_op jit(solution)/shard_map/while/body/eval_jaxpr/dot_general | solution.py:130
  673.1 39.4 %select_subtract_fusion.2 = (f32[128,2048]{1,0:T(8,128)S(1)}, f32[128,2048]{1,0:T(8,128)S(1)}) fusion(f32[128,2048]{1,0:T(8,128)S(1)} %copy-done.5, f32[128,2048]{1,0:T(8,128)} %fusion.61, f32[2048]{0:T(1024)S(1)} %get-tuple-element.673, f32[2048]{0:T(1024)S(1)} %get-tuple-element.674, pred[]{:T(512)S(6)} %compare.28, ...), kind=kOutput, calls=%fused_computation.22.clone.1 | convolution fusion | flops 3253207040 | bytes 5791749 | tf_op jit(solution)/shard_map/while/body/eval_jaxpr/dot_general | solution.py:123
  723.5 24.2 %all-to-all-done.1 = bf16[128,2,2048]{0,1,2:T(2,128)(2,1)S(1)} async-done(((bf16[128,2,2048]{0,1,2:T(2,128)(2,1)}), bf16[128,2,2048]{0,1,2:T(2,128)(2,1)S(1)}, u32[]{:S(2)}, u32[]{:S(2)}) %all-to-all-start.1) | async-done | bytes 1048608 | tf_op jit(solution)/shard_map/all_to_all | solution.py:147
  761.3 19.2 %reduce_window.7 = f32[512,512]{0,1:T(8,128)} reduce-window(f32[512,576]{0,1:T(8,128)S(1)} %maximum_convert_fusion, f32[]{:T(128)} %constant.320.clone.1), window={size=1x65}, to_apply=%region_2.3 | reduce-window | flops 16777216 | bytes 2228228 | tf_op jit(solution)/shard_map/reduce_window | solution.py:54
  817.8 15.2 %copy.47 = f32[1,8,512,1024]{3,1,2,0:T(8,128)S(1)} copy(f32[1,8,512,1024]{3,2,1,0:T(8,128)} %pad_bitcast_fusion.1) | data formatting | bytes 33554432
  851.7 17.2 %reshape.249 = f32[8,512,1023]{2,1,0:T(8,128)} reshape(f32[4190208]{0:T(1024)} %reshape.256) | data formatting | bytes 33521664 | tf_op jit(solution)/shard_map/reshape | solution.py:74
  884.6 422.7 %while.40 = (s32[]{:T(128)}, f32[8,8192]{1,0:T(8,128)S(1)}, bf16[512,1024]{1,0:T(8,128)(2,1)S(1)}, s32[]{:T(128)}, s32[]{:T(128)}, /*index=5*/bf16[4096]{0:T(102...) while((s32[]{:T(128)}, f32[8,8192]{1,0:T(8,128)S(1)}, ...), condition=%wide.region_6.7_spmd, body=%wide.region_4.6_spmd.sunk | while | flops 4299706368 | bytes 217369840 | solution.py:197
  928.7 15.2 %copy.54 = f32[1,8,512,1024]{3,1,2,0:T(8,128)S(1)} copy(f32[1,8,512,1024]{3,2,1,0:T(8,128)} %pad_bitcast_fusion.3) | data formatting | bytes 33554432 | tf_op jit(solution)/shard_map/while
  962.5 17.2 %reshape.261 = f32[8,512,1023]{2,1,0:T(8,128)} reshape(f32[4190208]{0:T(1024)} %reshape.260) | data formatting | bytes 33521664 | tf_op jit(solution)/shard_map/while/body/eval_jaxpr/reshape | solution.py:74
  1034.7 15.2 %copy.54 = f32[1,8,512,1024]{3,1,2,0:T(8,128)S(1)} copy(f32[1,8,512,1024]{3,2,1,0:T(8,128)} %pad_bitcast_fusion.3) | data formatting | bytes 33554432 | tf_op jit(solution)/shard_map/while
  1068.6 17.2 %reshape.261 = f32[8,512,1023]{2,1,0:T(8,128)} reshape(f32[4190208]{0:T(1024)} %reshape.260) | data formatting | bytes 33521664 | tf_op jit(solution)/shard_map/while/body/eval_jaxpr/reshape | solution.py:74
  1140.9 15.2 %copy.54 = f32[1,8,512,1024]{3,1,2,0:T(8,128)S(1)} copy(f32[1,8,512,1024]{3,2,1,0:T(8,128)} %pad_bitcast_fusion.3) | data formatting | bytes 33554432 | tf_op jit(solution)/shard_map/while
  1174.7 17.2 %reshape.261 = f32[8,512,1023]{2,1,0:T(8,128)} reshape(f32[4190208]{0:T(1024)} %reshape.260) | data formatting | bytes 33521664 | tf_op jit(solution)/shard_map/while/body/eval_jaxpr/reshape | solution.py:74
  1247.1 15.2 %copy.54 = f32[1,8,512,1024]{3,1,2,0:T(8,128)S(1)} copy(f32[1,8,512,1024]{3,2,1,0:T(8,128)} %pad_bitcast_fusion.3) | data formatting | bytes 33554432 | tf_op jit(solution)/shard_map/while
  1280.9 17.2 %reshape.261 = f32[8,512,1023]{2,1,0:T(8,128)} reshape(f32[4190208]{0:T(1024)} %reshape.260) | data formatting | bytes 33521664 | tf_op jit(solution)/shard_map/while/body/eval_jaxpr/reshape | solution.py:74
  1308.3 133.7 %reduce-scatter.2.cloned.1.call-done = f32[8,256]{1,0:T(8,128)} async-done(((f32[8,8192]{1,0:T(8,128)}), f32[8,256]{1,0:T(8,128)}) %reduce-scatter.2.cloned.1.call-update) | async-done | bytes 8208 | tf_op jit(solution)/shard_map/reduce_scatter | solution.py:198
  (170 shorter events, 411.9 us)
Async XLA Ops:
  10.6 54.8 %all-to-all-start = ((bf16[256,32,128]{2,0,1:T(8,128)(2,1)}), bf16[256,32,128]{2,0,1:T(8,128)(2,1)S(1)}, u32[]{:S(2)}, u32[]{:S(2)}) async-start(bf16[256,32,128]{2,0,1:T(8,128)(2,1)} %copy_bitcast_fusion), calls=%async_computation | async-start | bytes 4194304 | tf_op jit(solution)/shard_map/all_to_all | solution.py:106
  67.8 40.3 %copy-start.5 = (f32[128,2048]{1,0:T(8,128)S(1)}, f32[128,2048]{1,0:T(8,128)}, u32[]{:S(2)}) copy-start(f32[128,2048]{1,0:T(8,128)} %get-tuple-element.688) | copy-start | bytes 3145732 | tf_op jit(solution)/shard_map/while
  147.6 1.0 copy-start.6
  148.5 40.3 %copy-start.5 = (f32[128,2048]{1,0:T(8,128)S(1)}, f32[128,2048]{1,0:T(8,128)}, u32[]{:S(2)}) copy-start(f32[128,2048]{1,0:T(8,128)} %get-tuple-element.688) | copy-start | bytes 3145732 | tf_op jit(solution)/shard_map/while
  228.3 1.0 copy-start.6
  229.3 40.3 %copy-start.5 = (f32[128,2048]{1,0:T(8,128)S(1)}, f32[128,2048]{1,0:T(8,128)}, u32[]{:S(2)}) copy-start(f32[128,2048]{1,0:T(8,128)} %get-tuple-element.688) | copy-start | bytes 3145732 | tf_op jit(solution)/shard_map/while
  309.0 1.0 copy-start.6
  310.0 40.3 %copy-start.5 = (f32[128,2048]{1,0:T(8,128)S(1)}, f32[128,2048]{1,0:T(8,128)}, u32[]{:S(2)}) copy-start(f32[128,2048]{1,0:T(8,128)} %get-tuple-element.688) | copy-start | bytes 3145732 | tf_op jit(solution)/shard_map/while
  389.7 1.0 copy-start.6
  390.7 40.3 %copy-start.5 = (f32[128,2048]{1,0:T(8,128)S(1)}, f32[128,2048]{1,0:T(8,128)}, u32[]{:S(2)}) copy-start(f32[128,2048]{1,0:T(8,128)} %get-tuple-element.688) | copy-start | bytes 3145732 | tf_op jit(solution)/shard_map/while
  470.4 1.0 copy-start.6
  471.4 40.3 %copy-start.5 = (f32[128,2048]{1,0:T(8,128)S(1)}, f32[128,2048]{1,0:T(8,128)}, u32[]{:S(2)}) copy-start(f32[128,2048]{1,0:T(8,128)} %get-tuple-element.688) | copy-start | bytes 3145732 | tf_op jit(solution)/shard_map/while
  551.1 1.0 copy-start.6
  552.1 40.3 %copy-start.5 = (f32[128,2048]{1,0:T(8,128)S(1)}, f32[128,2048]{1,0:T(8,128)}, u32[]{:S(2)}) copy-start(f32[128,2048]{1,0:T(8,128)} %get-tuple-element.688) | copy-start | bytes 3145732 | tf_op jit(solution)/shard_map/while
  631.8 1.0 copy-start.6
  632.8 40.3 %copy-start.5 = (f32[128,2048]{1,0:T(8,128)S(1)}, f32[128,2048]{1,0:T(8,128)}, u32[]{:S(2)}) copy-start(f32[128,2048]{1,0:T(8,128)} %get-tuple-element.688) | copy-start | bytes 3145732 | tf_op jit(solution)/shard_map/while
  712.5 1.0 copy-start.6
  717.0 30.6 %all-to-all-start.1 = ((bf16[128,2,2048]{0,1,2:T(2,128)(2,1)}), bf16[128,2,2048]{0,1,2:T(2,128)(2,1)S(1)}, u32[]{:S(2)}, u32[]{:S(2)}) async-start(bf16[128,2,2048]{0,1,2:T(2,128)(2,1)} %copy.35), calls=%async_computation.1 | async-start | bytes 2097152 | tf_op jit(solution)/shard_map/all_to_all | solution.py:147
  721.4 720.6 %reduce-scatter.2.cloned.1.call-start = ((), (), s32[]{:S(2)}) async-start(), calls=%async_computation.3 | async-start | bytes 270336 | tf_op jit(solution)/shard_map/reduce_scatter | solution.py:198
  753.0 3.4 collective-permute-start.1
  754.3 5.8 collective-permute-start.2
  796.0 1.9 copy-start
  796.0 3.2 copy-start.1
  868.9 7.3 copy-start.2
  884.6 423.5 %copy-start.7 = (s32[8,8]{1,0:T(8,128)S(1)}, s32[8,8]{1,0:T(8,128)}, u32[]{:S(2)}) copy-start(s32[8,8]{1,0:T(8,128)} %iota_subtract_fusion) | copy-start | bytes 772
  884.6 423.5 %copy-start.8 = (s32[8,8]{1,0:T(8,128)S(1)}, s32[8,8]{1,0:T(8,128)}, u32[]{:S(2)}) copy-start(s32[8,8]{1,0:T(8,128)} %param.7) | copy-start | bytes 772
  884.6 423.5 %copy-start.10 = (s32[15]{0:T(128)S(1)}, s32[15]{0:T(128)}, u32[]{:S(2)}) copy-start(s32[15]{0:T(128)} %iota_add_fusion.2) | copy-start | bytes 184
  884.6 423.6 %copy-start.9 = (s32[256]{0:T(256)S(1)}, s32[256]{0:T(256)}, u32[]{:S(2)}) copy-start(s32[256]{0:T(256)} %add_add_fusion) | copy-start | bytes 3076
  884.8 13.0 collective-permute-start
  988.9 15.0 %collective-permute-start = (bf16[512,1024]{1,0:T(8,128)(2,1)S(1)}, bf16[512,1024]{1,0:T(8,128)(2,1)S(1)}, u32[]{:S(2)}, u32[]{:S(2)}) collective-permute-start(bf16[512,1024]{1,0:T(8,128)(2,1)S(1)} %get-tuple-element.727), channel_id=1, source_target_pairs={{0,28},{4,0},{8,4},{12,8},{16,12},{20,16},{24,20},{28,24},{1,29},{... | collective-permute-start | bytes 3145736 | tf_op jit(solution)/shard_map/while/body/eval_jaxpr/ppermute | solution.py:37
  1094.9 15.1 %collective-permute-start = (bf16[512,1024]{1,0:T(8,128)(2,1)S(1)}, bf16[512,1024]{1,0:T(8,128)(2,1)S(1)}, u32[]{:S(2)}, u32[]{:S(2)}) collective-permute-start(bf16[512,1024]{1,0:T(8,128)(2,1)S(1)} %get-tuple-element.727), channel_id=1, source_target_pairs={{0,28},{4,0},{8,4},{12,8},{16,12},{20,16},{24,20},{28,24},{1,29},{... | collective-permute-start | bytes 3145736 | tf_op jit(solution)/shard_map/while/body/eval_jaxpr/ppermute | solution.py:37
  1201.1 15.2 %collective-permute-start = (bf16[512,1024]{1,0:T(8,128)(2,1)S(1)}, bf16[512,1024]{1,0:T(8,128)(2,1)S(1)}, u32[]{:S(2)}, u32[]{:S(2)}) collective-permute-start(bf16[512,1024]{1,0:T(8,128)(2,1)S(1)} %get-tuple-element.727), channel_id=1, source_target_pairs={{0,28},{4,0},{8,4},{12,8},{16,12},{20,16},{24,20},{28,24},{1,29},{... | collective-permute-start | bytes 3145736 | tf_op jit(solution)/shard_map/while/body/eval_jaxpr/ppermute | solution.py:37
  (2 other events, 1.5 us)
Sparse Core Ops, SparseCore 0:
  1308.1 133.7 reduce-scatter.1
where the time goes:
time: 1460 us; the launch traced here: 1450 us
  matrix products  685 us (47%)
  local copies, waits for them, and re-layouts  386 us (26%)
  waiting for transfers between devices  258 us (18%)
  other arithmetic  82.5 us (6%)
  starting transfers between devices  23.5 us (2%)
    dot_general x8, matrix products, transform_block(): lax.dot_general(samples, base_sin, dims, precision=lax.Precision.HIGHEST,...  322 us
    dot_general x8, matrix products, transform_block(): lax.dot_general(samples, base_cos, dims, precision=lax.Precision.HIGHEST,...  316 us
    while x52, local copies, waits for them, and re-layouts  168 us
    reduce_scatter x1, waiting for transfers between devices, on_device(): lax.psum_scatter(total, ('blk', 'lag'), scatter_dimension=1, tiled=True)  134 us
    reshape x5, local copies, waits for them, and re-layouts, diagonal_sums(): return jnp.sum(flat.reshape(product.shape[0], rows, width), axis=1)  86 us
    ppermute x4, waiting for transfers between devices, from_behind(): return lax.ppermute(value, axis, pairs)  49 us
    dot_general x5, matrix products, contribution(): lax.dot_general(rotated, piece * live[:, None], (((1,), (1,)), ((), ())),...  48 us
    all_to_all x1, waiting for transfers between devices, on_device(): lax.all_to_all(raw.astype(jnp.bfloat16), ('blk', 'lag'), split_axis=1, co...  47.5 us
  transfers between devices with their start and end apart: 9, of which 8 were waited for; matrix products, arithmetic and copies ran while one was open for 0% of the time, Pallas kernels for 0%

commit v1 on v0

v1 whole, which is shorter than its diff:
```python
import functools
import math

import jax
import jax.numpy as jnp
import ml_dtypes
import numpy as np
from jax import lax
from jax.experimental import pallas as pl
from jax.experimental.pallas import tpu as pltpu
from jax.sharding import PartitionSpec as P

NT = 8192
C = 4096
NB = 2048
K0 = 16
SW = 32
TAPER = 128
LAGS = 8
LAG_STEP = 32
EPS = 1e-06

RADIX = 16
SPAN = NT // RADIX
M_ROWS = NB // RADIX
LANES = 128
PAD = 8
bf16 = ml_dtypes.bfloat16


def split_high_low(table):
    high = table.astype(bf16)
    low = (table - high.astype(np.float64)).astype(bf16)
    return high, low


@functools.cache
def spectrum_tables():
    m = np.arange(M_ROWS)[:, None] + 1
    s = np.arange(SPAN)[None, :]

    def waves(rho):
        angle = 2 * np.pi * (((RADIX * m + rho) * s) % NT) / NT
        return np.cos(angle), np.sin(angle)

    zero = np.zeros((M_ROWS, SPAN))
    tables = []
    c0, s0 = waves(0)
    c8, s8 = waves(RADIX // 2)
    tables.append(np.block([[c0, zero], [-s0, zero], [zero, c8], [zero, -s8]]))
    for rho in range(1, RADIX // 2):
        ca, sa = waves(rho)
        cb, sb = waves(RADIX - rho)
        tables.append(np.block([[ca, sa], [-sa, ca], [cb, -sb], [-sb, -cb]]))
    return np.stack(tables).astype(bf16)


@functools.cache
def taper_table():
    j = np.arange(NB, dtype=np.float64)
    edge = np.minimum(j, NB - 1 - j)
    weights = np.where(edge < TAPER, 0.5 - 0.5 * np.cos(math.pi * (edge + 0.5) / TAPER), 1.0)
    weights = weights.reshape(M_ROWS, RADIX).T
    return np.ascontiguousarray(weights.astype(np.float32)[:, :, None])


@functools.cache
def channel_tables(width, chunk):
    size = 2 * width
    c = np.arange(width)[:, None]
    q = np.arange(size)[None, :]
    angle = 2 * np.pi * ((c * q) % size) / size
    both = np.stack([np.cos(angle), np.sin(angle)], axis=1).reshape(width, 2, size // chunk, chunk)
    both = both.transpose(2, 0, 1, 3).reshape(size // chunk, width, 2 * chunk)
    return split_high_low(both)


@functools.cache
def offset_tables(width, chunk):
    size = 2 * width
    q = np.arange(size)[:, None]
    d = np.arange(size)[None, :] - width
    angle = 2 * np.pi * ((q * d) % size) / size
    both = np.stack([np.cos(angle), np.sin(angle)]) / size
    both[:, :, 0] = 0.0
    both = both.reshape(2, size // chunk, chunk, size).transpose(1, 0, 2, 3)
    return split_high_low(both.reshape(size // chunk, 2 * chunk, size))


def real_dft16(x):
    a = [x[h] + x[h + 8] for h in range(8)]
    b = [x[h] - x[h + 8] for h in range(8)]
    out = {}
    lo = [a[h] + a[h + 4] for h in range(4)]
    d = [a[h] - a[h + 4] for h in range(4)]
    out[0] = (lo[0] + lo[2]) + (lo[1] + lo[3])
    out[8] = (lo[0] + lo[2]) - (lo[1] + lo[3])
    out[4] = (lo[0] - lo[2], lo[3] - lo[1])
    root = math.sqrt(0.5)
    minus, plus = (d[1] - d[3]) * root, (d[1] + d[3]) * root
    out[2] = (d[0] + minus, -(d[2] + plus))
    out[6] = (d[0] - minus, d[2] - plus)
    diff = [None] + [b[h] - b[8 - h] for h in range(1, 4)]
    add = [None] + [b[h] + b[8 - h] for h in range(1, 4)]
    for rho in (1, 3, 5, 7):
        re, im = b[0], b[4] * (-math.sin(math.pi * rho / 2))
        for h in range(1, 4):
            re = re + diff[h] * math.cos(math.pi * h * rho / 8)
            im = im - add[h] * math.sin(math.pi * h * rho / 8)
        out[rho] = (re, im)
    return out


def whiten_kernel(groups, series_ref, table_ref, taper_ref, white_ref, y_ref, spec_ref, pre_ref, suf_ref, all_ref):
    step = pl.program_id(0)
    half = RADIX // 2
    rows = 16

    @pl.when(step == 0)
    def _():
        @pl.loop(0, SPAN // rows)
        def _(i):
            start = pl.multiple_of(i * rows, rows)
            x = [
                series_ref[pl.ds(pl.multiple_of(h * SPAN + start, rows), rows), :].astype(jnp.float32)
                for h in range(RADIX)
            ]
            y = real_dft16(x)
            y[0] = (y[0], y[half])
            for rho in range(half):
                for part in range(2):
                    y_ref[rho, pl.ds(pl.multiple_of(part * SPAN + start, rows), rows), :] = y[rho][part].astype(
                        jnp.bfloat16
                    )

    both = jnp.dot(table_ref[0], y_ref[step], preferred_element_type=jnp.float32)
    other = jnp.where(step == 0, half, RADIX - step)
    spec_ref[step] = both[: 2 * M_ROWS]
    spec_ref[other] = both[2 * M_ROWS :]

    @pl.when(step == half - 1)
    def _():
        chans = series_ref.shape[1]
        edge = jnp.zeros((PAD, chans), jnp.float32)
        inner = pl.ds(PAD, M_ROWS)

        def amplitude(rho):
            re = spec_ref[rho, pl.ds(0, M_ROWS), :]
            im = spec_ref[rho, pl.ds(M_ROWS, M_ROWS), :]
            return jnp.sqrt(re * re + im * im)

        for ref, order in ((pre_ref, range(RADIX)), (suf_ref, range(RADIX - 1, -1, -1))):
            for n, rho in enumerate(order):
                ref[rho, pl.ds(0, PAD), :] = edge
                ref[rho, pl.ds(PAD + M_ROWS, PAD), :] = edge
                if ref is pre_ref:
                    amp = amplitude(rho)
                    spec_amp = amp if n == 0 else ref[rho - 1, inner, :] + amp
                    ref[rho, inner, :] = spec_amp
                    suf_ref[rho, inner, :] = amp
                elif n > 0:
                    ref[rho, inner, :] = ref[rho, inner, :] + ref[rho + 1, inner, :]
        last = RADIX - 1
        all_ref[...] = (
            pre_ref[last, pl.ds(PAD - 1, M_ROWS), :]
            + pre_ref[last, inner, :]
            + pre_ref[last, pl.ds(PAD + 1, M_ROWS), :]
        )
        per = M_ROWS // groups
        for rho in range(RADIX):
            total = all_ref[...] + suf_ref[rho, pl.ds(PAD - 2, M_ROWS), :] + pre_ref[rho, pl.ds(PAD + 2, M_ROWS), :]
            scale = taper_ref[rho] / (total / (2 * SW + 1) + EPS)
            for part in range(2):
                value = (spec_ref[rho, pl.ds(part * M_ROWS, M_ROWS), :] * scale).astype(jnp.bfloat16)
                for g in range(groups):
                    white_ref[rho * groups + g, part] = value[g * per : (g + 1) * per]


def whiten(series, n_dev):
    chans = series.shape[1]
    groups = n_dev // RADIX
    half = RADIX // 2
    out = jax.ShapeDtypeStruct((n_dev, 2, M_ROWS // groups, chans), jnp.bfloat16)
    return pl.pallas_call(
        functools.partial(whiten_kernel, groups),
        grid=(half,),
        out_shape=out,
        in_specs=[
            pl.BlockSpec(series.shape, lambda i: (0, 0)),
            pl.BlockSpec((1, 4 * M_ROWS, 2 * SPAN), lambda i: (i, 0, 0)),
            pl.BlockSpec((RADIX, M_ROWS, 1), lambda i: (0, 0, 0)),
        ],
        out_specs=pl.BlockSpec(out.shape, lambda i: (0, 0, 0, 0)),
        scratch_shapes=[
            pltpu.VMEM((half, 2 * SPAN, chans), jnp.bfloat16),
            pltpu.VMEM((RADIX, 2 * M_ROWS, chans), jnp.float32),
            pltpu.VMEM((RADIX, M_ROWS + 2 * PAD, chans), jnp.float32),
            pltpu.VMEM((RADIX, M_ROWS + 2 * PAD, chans), jnp.float32),
            pltpu.VMEM((M_ROWS, chans), jnp.float32),
        ],
        compiler_params=pltpu.CompilerParams(vmem_limit_bytes=40 * 2**20),
        cost_estimate=pl.CostEstimate(flops=2 * 8 * 512 * 1024 * chans, bytes_accessed=12 * 2**20, transcendentals=0),
        name="whiten",
    )(series, jnp.asarray(spectrum_tables()), jnp.asarray(taper_table()))


def split_rounded(value):
    high = value.astype(jnp.bfloat16)
    return high, (value - high.astype(jnp.float32)).astype(jnp.bfloat16)


def correlate_kernel(
    blocks, mask_ref, white_ref, waves_ref, high_ref, low_ref, back_high_ref, back_low_ref, out_ref, lhs_ref, re_ref, im_ref, h_ref, acc_ref
):
    step = pl.program_id(0)
    sources, _, bins, chans = white_ref.shape
    per_block = sources // blocks
    chunk = re_ref.shape[2]
    width = per_block * chans
    f32 = jnp.float32

    @pl.when(step == 0)
    def _():
        acc_ref[...] = jnp.zeros_like(acc_ref)
        for s in range(sources):
            block, place = divmod(s, per_block)
            for part in range(2):
                lhs_ref[pl.ds((2 * block + part) * bins, bins), pl.ds(place * chans, chans)] = white_ref[s, part]

    for block in range(blocks):
        lhs = lhs_ref[pl.ds(2 * block * bins, 2 * bins), :]
        product = jnp.dot(lhs, high_ref[0], preferred_element_type=f32)
        product = product + jnp.dot(lhs, low_ref[0], preferred_element_type=f32)
        re_ref[block] = product[:bins, :chunk] + product[bins:, chunk:]
        im_ref[block] = product[bins:, :chunk] - product[:bins, chunk:]

    half = LAGS // 2
    zero_row = (blocks - 1) * LAGS
    for delta in range(blocks):
        sums = [jnp.zeros((8, chunk), f32) for _ in range(4 * half)]
        for b in range(bins // 8):
            rows = pl.ds(8 * b, 8)
            g_re = jnp.zeros((8, chunk), f32)
            g_im = jnp.zeros((8, chunk), f32)
            for block in range(blocks - delta):
                keep = mask_ref[block, block + delta]
                a_re, a_im = re_ref[block, rows, :], im_ref[block, rows, :]
                if delta == 0:
                    g_re = g_re + keep * (a_re * a_re + a_im * a_im)
                else:
                    b_re, b_im = re_ref[block + delta, rows, :], im_ref[block + delta, rows, :]
                    g_re = g_re + keep * (a_re * b_re + a_im * b_im)
                    g_im = g_im + keep * (a_im * b_re - a_re * b_im)
            for j in range(half):
                cosine, sine = waves_ref[j, rows, :], waves_ref[half + j, rows, :]
                sums[4 * j] = sums[4 * j] + cosine * g_re
                sums[4 * j + 1] = sums[4 * j + 1] + sine * g_re
                if delta > 0:
                    sums[4 * j + 2] = sums[4 * j + 2] + cosine * g_im
                    sums[4 * j + 3] = sums[4 * j + 3] + sine * g_im
        sums = [jnp.sum(value, axis=0, keepdims=True) for value in sums]
        h_re, h_im = [None] * LAGS, [None] * LAGS
        for j in range(half):
            cr, sr, ci, si = sums[4 * j : 4 * j + 4]
            h_re[half + j], h_im[half + j] = cr - si, ci + sr
            h_re[half - 1 - j], h_im[half - 1 - j] = cr + si, ci - sr
        ahead = zero_row + delta * LAGS
        h_ref[pl.ds(ahead, LAGS), pl.ds(0, chunk)] = jnp.concatenate(h_re, axis=0)
        h_ref[pl.ds(ahead, LAGS), pl.ds(chunk, chunk)] = jnp.concatenate(h_im, axis=0)
        if delta > 0:
            behind = zero_row - delta * LAGS
            h_ref[pl.ds(behind, LAGS), pl.ds(0, chunk)] = jnp.concatenate(h_re[::-1], axis=0)
            h_ref[pl.ds(behind, LAGS), pl.ds(chunk, chunk)] = -jnp.concatenate(h_im[::-1], axis=0)

    h_high, h_low = split_rounded(h_ref[...])
    acc_ref[...] += (
        jnp.dot(h_high, back_high_ref[0], preferred_element_type=f32)
        + jnp.dot(h_low, back_high_ref[0], preferred_element_type=f32)
        + jnp.dot(h_high, back_low_ref[0], preferred_element_type=f32)
    )

    @pl.when(step == pl.num_programs(0) - 1)
    def _():
        devices, _, cols = out_ref.shape
        parts = width // cols
        for segment in range(2 * blocks):
            value = jnp.zeros((LAGS, width), f32)
            if segment < 2 * blocks - 1:
                value = value + acc_ref[pl.ds(segment * LAGS, LAGS), pl.ds(0, width)]
            if segment > 0:
                value = value + acc_ref[pl.ds((segment - 1) * LAGS, LAGS), pl.ds(width, width)]
            for part in range(parts):
                out_ref[segment * parts + part] = value[:, part * cols : (part + 1) * cols]


def correlate(white, mask, waves):
    n_dev, _, bins, chans = white.shape
    blocks = mask.shape[0]
    width = C // blocks
    size = 2 * width
    chunk = LANES
    high, low = channel_tables(width, chunk)
    back_high, back_low = offset_tables(width, chunk)
    rows = (2 * blocks - 1) * LAGS
    out = jax.ShapeDtypeStruct((n_dev, LAGS, 2 * C // n_dev), jnp.float32)
    table = pl.BlockSpec((1, width, 2 * chunk), lambda i: (i, 0, 0))
    back = pl.BlockSpec((1, 2 * chunk, size), lambda i: (i, 0, 0))
    return pl.pallas_call(
        functools.partial(correlate_kernel, blocks),
        grid=(size // chunk,),
        out_shape=out,
        in_specs=[
            pl.BlockSpec(memory_space=pltpu.SMEM),
            pl.BlockSpec(white.shape, lambda i: (0, 0, 0, 0)),
            pl.BlockSpec(waves.shape, lambda i: (0, 0, 0)),
            table,
            table,
            back,
            back,
        ],
        out_specs=pl.BlockSpec(out.shape, lambda i: (0, 0, 0)),
        scratch_shapes=[
            pltpu.VMEM((blocks * 2 * bins, width), jnp.bfloat16),
            pltpu.VMEM((blocks, bins, chunk), jnp.float32),
            pltpu.VMEM((blocks, bins, chunk), jnp.float32),
            pltpu.VMEM((rows, 2 * chunk), jnp.float32),
            pltpu.VMEM((rows, size), jnp.float32),
        ],
        compiler_params=pltpu.CompilerParams(vmem_limit_bytes=40 * 2**20),
        cost_estimate=pl.CostEstimate(flops=5 * 2**30, bytes_accessed=14 * 2**20, transcendentals=0),
        name="correlate",
    )(
        mask.astype(jnp.float32),
        white,
        waves,
        jnp.asarray(high),
        jnp.asarray(low),
        jnp.asarray(back_high),
        jnp.asarray(back_low),
    )


def lag_waves(device, bins, groups):
    rho, group = device // groups, device % groups
    k = RADIX * (group * bins + lax.iota(jnp.int32, bins) + 1) + rho
    number = lax.iota(jnp.int32, LAGS // 2) + LAGS // 2
    shifts = LAG_STEP * (2 * number + 1 - LAGS) // 2
    phase = jnp.mod(shifts[:, None] * k[None, :], NT).astype(jnp.float32) * (2 * math.pi / NT)
    waves = jnp.concatenate([jnp.cos(phase), jnp.sin(phase)], axis=0)
    return jnp.broadcast_to(waves[:, :, None], (LAGS, bins, LANES))


def pair_counts(mask, columns):
    blocks = mask.shape[0]
    width = C // blocks
    labels = lax.iota(jnp.int32, blocks)
    apart = labels[None, :] - labels[:, None]
    deltas = lax.iota(jnp.int32, 2 * blocks - 1) - (blocks - 1)
    per_delta = jnp.sum(
        mask[None] * (apart[None] == deltas[:, None, None]).astype(jnp.int32), axis=(1, 2)
    )
    offsets = columns - C
    intersection = jnp.maximum(0, width - jnp.abs(offsets[:, None] - width * deltas[None, :]))
    return jnp.sum(intersection * per_delta[None, :], axis=1)


def stack_scale(counts):
    return 1.0 / jnp.sqrt(NB * jnp.maximum(counts, 1).astype(jnp.float32))


def on_device(raw, mask):
    axes = ("blk", "lag")
    n_dev = lax.axis_size("blk") * lax.axis_size("lag")
    device = lax.axis_index("blk") * lax.axis_size("lag") + lax.axis_index("lag")
    series = lax.all_to_all(raw.astype(jnp.bfloat16), axes, split_axis=1, concat_axis=0, tiled=True)
    white = whiten(series, n_dev)
    waves = lag_waves(device, white.shape[2], n_dev // RADIX)
    white = lax.all_to_all(white, axes, split_axis=0, concat_axis=0, tiled=True)
    partial = correlate(white, mask, waves)
    shares = lax.all_to_all(partial, axes, split_axis=0, concat_axis=0, tiled=True)
    total = jnp.sum(shares, axis=0)
    n_cols = total.shape[1]
    counts = pair_counts(mask, device * n_cols + lax.iota(jnp.int32, n_cols))
    return total * stack_scale(counts)[None, :]


def solution(mesh):
    return jax.shard_map(
        on_device,
        mesh=mesh,
        in_specs=(P(("blk", "lag"), None), P()),
        out_specs=P(None, ("blk", "lag")),
        check_vma=False,
    )
```

time: 1460 us -> 132 us (0.09)
  matrix products: 685 us -> 0 us
  local copies, waits for them, and re-layouts: 386 us -> 6.1 us
  waiting for transfers between devices: 258 us -> 34.8 us
  other arithmetic: 82.5 us -> 3.86 us
  blocking collectives: 0 us -> 54.6 us
  Pallas kernels: 0 us -> 22.9 us
    dot_general x21 -> x0, matrix products: 685 us -> none  [the longest x8 322 us: transform_block(): lax.dot_general(samples, base_sin, dims, precision=lax.Precision.HIGHEST,...]
    while x53 -> x0, local copies, waits for them, and re-layouts: 168 us -> none
    reduce_scatter x1 -> x0, waiting for transfers between devices: 134 us -> none  [on_device(): lax.psum_scatter(total, ('blk', 'lag'), scatter_dimension=1, tiled=True)]
    reshape x9 -> x0, local copies, waits for them, and re-layouts: 122 us -> none  [the longest x5 86 us: diagonal_sums(): return jnp.sum(flat.reshape(product.shape[0], rows, width), axis=1)]
    all_to_all x0 -> x1, blocking collectives: none -> 54.6 us  [on_device(): lax.all_to_all(raw.astype(jnp.bfloat16), axes, split_axis=1, concat_axis=...]
    ppermute x6 -> x0, waiting for transfers between devices: 52.7 us -> none  [the longest x4 49 us: from_behind(): return lax.ppermute(value, axis, pairs)]
    unnamed x23 -> x14, local copies, waits for them, and re-layouts: 44.2 us -> 5.98 us
    all_to_all x2, waiting for transfers between devices: 71.6 us -> 34.8 us  [the longest x1 24.8 us: on_device(): white = lax.all_to_all(white, axes, split_axis=0, concat_axis=0, tiled=True)]
  transfers between devices with their start and end apart: 9 -> 2, of which waited for: 8 -> 2; matrix products, arithmetic and copies ran while one was open for 0% -> 0% of each run, Pallas kernels for 0% -> 0%
where the time goes in v1:
time: 132 us; the launch traced here: 131 us
  blocking collectives  54.6 us (41%)
  waiting for transfers between devices  34.8 us (26%)
  Pallas kernels  22.9 us (17%)
  starting transfers between devices  8.92 us (7%)
  local copies, waits for them, and re-layouts  6.1 us (5%)
  other arithmetic  3.86 us (3%)
    all_to_all x1, blocking collectives, on_device(): lax.all_to_all(raw.astype(jnp.bfloat16), axes, split_axis=1, concat_axis=...  54.6 us
    all_to_all x1, waiting for transfers between devices, on_device(): white = lax.all_to_all(white, axes, split_axis=0, concat_axis=0, tiled=True)  24.8 us
    pallas_call x1, Pallas kernels, correlate(): pl.pallas_call(functools.partial(correlate_kernel, blocks), grid=(size //...  16.1 us
    all_to_all x1, waiting for transfers between devices, on_device(): lax.all_to_all(partial, axes, split_axis=0, concat_axis=0, tiled=True)  9.98 us
    pallas_call x1, Pallas kernels, whiten(): pl.pallas_call(functools.partial(whiten_kernel, groups), grid=(half,), ou...  6.82 us
    unnamed x14, local copies, waits for them, and re-layouts  5.98 us
    all_to_all x1, starting transfers between devices, on_device(): lax.all_to_all(partial, axes, split_axis=0, concat_axis=0, tiled=True)  4.46 us
    all_to_all x1, starting transfers between devices, on_device(): white = lax.all_to_all(white, axes, split_axis=0, concat_axis=0, tiled=True)  4.45 us
  transfers between devices with their start and end apart: 2, of which 2 were waited for; matrix products, arithmetic and copies ran while one was open for 0% of the time, Pallas kernels for 0%

profile of v1, /device:TPU:0, one launch (start us, length us, event | category | flops | bytes accessed | tf_op | source)
XLA Modules:
  0.0 131.4 jit_solution(2932764737353980667)
XLA Ops:
  0.0 0.0 copy-start
  0.0 2.8 %copy_bitcast_fusion = bf16[256,32,128]{2,0,1:T(8,128)(2,1)S(1)} fusion(f32[256,4096]{1,0:T(8,128)} %param.8), kind=kLoop, calls=%fused_computation | loop fusion | flops 1048576 | bytes 6291456 | tf_op jit(solution)/shard_map/all_to_all | solution.py:375
  2.9 0.0 copy-start.1
  2.9 54.6 %all_to_all.29 = bf16[256,32,128]{2,0,1:T(8,128)(2,1)S(1)} all-to-all(bf16[256,32,128]{2,0,1:T(8,128)(2,1)S(1)} %copy_bitcast_fusion), channel_id=1, replica_groups=mesh['blk'=8,'lag'=4] {'blk','lag'}, dimensions={1} | all-to-all | bytes 4194304 | tf_op jit(solution)/shard_map/all_to_all | solution.py:375
  57.5 0.0 copy-done
  57.5 0.0 copy-done.1
  57.5 6.8 %whiten.1 = bf16[32,2,64,128]{3,2,1,0:T(8,128)(2,1)} custom-call(bf16[8192,128]{1,0:T(8,128)(2,1)S(1)} %bitcast.8, bf16[8,512,1024]{2,1,0:T(8,128)(2,1)S(1)} %copy-done, f32[16,128,1]{2,1,0:T(8,128)S(1)} %copy-done.1), custom_call_target="tpu_custom_call" | custom-call | flops 1073741824 | bytes 12582912 | tf_op jit(solution)/shard_map/whiten/pallas_call | solution.py:184
  64.3 0.0 copy-start.6
  64.3 0.0 copy-start.4
  64.3 4.5 %all-to-all-start.1 = ((bf16[32,2,64,128]{3,2,1,0:T(8,128)(2,1)}), bf16[32,2,64,128]{3,2,1,0:T(8,128)(2,1)S(1)}, u32[]{:S(2)}, u32[]{:S(2)}) async-start(bf16[32,2,64,128]{3,2,1,0:T(8,128)(2,1)} %whiten.1), calls=%async_computation.1 | async-start | bytes 2097152 | tf_op jit(solution)/shard_map/all_to_all | solution.py:378
  68.8 0.0 copy-done.6
  68.9 0.1 fusion.4
  69.0 24.8 %all-to-all-done.1.white_ref = bf16[32,2,64,128]{3,2,1,0:T(8,128)(2,1)S(1)} async-done(((bf16[32,2,64,128]{3,2,1,0:T(8,128)(2,1)}), bf16[32,2,64,128]{3,2,1,0:T(8,128)(2,1)S(1)}, u32[]{:S(2)}, u32[]{:S(2)}) %all-to-all-start.1) | async-done | bytes 1048608 | tf_op jit(solution)/shard_map/all_to_all | solution.py:378
  93.8 0.1 broadcast_in_dim.2.waves_ref
  94.0 0.0 copy-done.4
  94.0 0.0 copy-start.2
  94.0 2.2 %copy-done.2 = bf16[8,256,1024]{2,1,0:T(8,128)(2,1)S(1)} copy-done((bf16[8,256,1024]{2,1,0:T(8,128)(2,1)S(1)}, bf16[8,256,1024]{2,1,0:T(8,128)(2,1)}, u32[]{:S(2)}) %copy-start.2) | copy-done | bytes 4194328
  96.2 0.0 copy-start.3
  96.2 2.2 %copy-done.3 = bf16[8,256,1024]{2,1,0:T(8,128)(2,1)S(1)} copy-done((bf16[8,256,1024]{2,1,0:T(8,128)(2,1)S(1)}, bf16[8,256,1024]{2,1,0:T(8,128)(2,1)}, u32[]{:S(2)}) %copy-start.3) | copy-done | bytes 4194328
  98.4 0.0 copy-start.5
  98.4 1.6 %copy-done.5 = bf16[8,512,256]{2,1,0:T(8,128)(2,1)S(1)} copy-done((bf16[8,512,256]{2,1,0:T(8,128)(2,1)S(1)}, bf16[8,512,256]{2,1,0:T(8,128)(2,1)}, u32[]{:S(2)}) %copy-start.5) | copy-done | bytes 2097176
  100.0 16.1 %correlate.1 = f32[32,8,256]{2,1,0:T(8,128)} custom-call(f32[8,8]{1,0:T(8,128)S(1)} %convert_element_type.17.mask_ref, bf16[32,2,64,128]{3,2,1,0:T(8,128)(2,1)S(1)} %all-to-all-done.1.white_ref, f32[8,64,128]{2,1,0:T(8,128)S(1)} %broadcast_in_dim.2.waves_ref, bf16[8,512,256]{2,1,0:T(8,128)(2,1)S(1)} %copy-done.4, bf16[8,512,256]{2,1,0:T(8,128)(2,1)S(1)} %copy-done.5, ...), custom_call_target="tpu_custom_call" | custom-call | flops 5368709120 | bytes 14680064 | tf_op jit(solution)/shard_map/correlate/pallas_call | solution.py:308
  116.1 4.5 %all-to-all-start.2 = ((f32[32,8,256]{2,1,0:T(8,128)}), f32[32,8,256]{2,1,0:T(8,128)S(1)}, u32[]{:S(2)}, u32[]{:S(2)}) async-start(f32[32,8,256]{2,1,0:T(8,128)} %correlate.1), calls=%async_computation.2 | async-start | bytes 524288 | tf_op jit(solution)/shard_map/all_to_all | solution.py:380
  120.5 0.1 select_reduce_fusion
  120.6 0.1 multiply_reduce_fusion
  120.7 10.0 %all-to-all-done.2 = f32[32,8,256]{2,1,0:T(8,128)S(1)} async-done(((f32[32,8,256]{2,1,0:T(8,128)}), f32[32,8,256]{2,1,0:T(8,128)S(1)}, u32[]{:S(2)}, u32[]{:S(2)}) %all-to-all-start.2) | async-done | bytes 262176 | tf_op jit(solution)/shard_map/all_to_all | solution.py:380
  130.8 0.6 broadcast_multiply_fusion
  (10 shorter events, 0.1 us)
Async XLA Ops:
  0.0 57.5 %copy-start = (bf16[8,512,1024]{2,1,0:T(8,128)(2,1)S(1)}, bf16[8,512,1024]{2,1,0:T(8,128)(2,1)}, u32[]{:S(2)}) copy-start(bf16[8,512,1024]{2,1,0:T(8,128)(2,1)} %constant.105.clone.table_ref) | copy-start | bytes 25165828
  2.9 54.7 %copy-start.1 = (f32[16,128,1]{2,1,0:T(8,128)S(1)}, f32[16,128,1]{2,1,0:T(8,128)}, u32[]{:S(2)}) copy-start(f32[16,128,1]{2,1,0:T(8,128)} %constant.106.clone.taper_ref) | copy-start | bytes 24580
  64.3 4.5 %copy-start.6 = (s32[8,8]{1,0:T(8,128)S(1)}, s32[8,8]{1,0:T(8,128)}, u32[]{:S(2)}) copy-start(s32[8,8]{1,0:T(8,128)} %param.9) | copy-start | bytes 772
  64.3 29.7 %copy-start.4 = (bf16[8,512,256]{2,1,0:T(8,128)(2,1)S(1)}, bf16[8,512,256]{2,1,0:T(8,128)(2,1)}, u32[]{:S(2)}) copy-start(bf16[8,512,256]{2,1,0:T(8,128)(2,1)} %constant.107.clone.high_ref) | copy-start | bytes 6291460
  64.3 29.5 %all-to-all-start.1 = ((bf16[32,2,64,128]{3,2,1,0:T(8,128)(2,1)}), bf16[32,2,64,128]{3,2,1,0:T(8,128)(2,1)S(1)}, u32[]{:S(2)}, u32[]{:S(2)}) async-start(bf16[32,2,64,128]{3,2,1,0:T(8,128)(2,1)} %whiten.1), calls=%async_computation.1 | async-start | bytes 2097152 | tf_op jit(solution)/shard_map/all_to_all | solution.py:378
  94.0 2.2 %copy-start.2 = (bf16[8,256,1024]{2,1,0:T(8,128)(2,1)S(1)}, bf16[8,256,1024]{2,1,0:T(8,128)(2,1)}, u32[]{:S(2)}) copy-start(bf16[8,256,1024]{2,1,0:T(8,128)(2,1)} %constant.109.clone.back_high_ref) | copy-start | bytes 12582916
  96.2 2.2 %copy-start.3 = (bf16[8,256,1024]{2,1,0:T(8,128)(2,1)S(1)}, bf16[8,256,1024]{2,1,0:T(8,128)(2,1)}, u32[]{:S(2)}) copy-start(bf16[8,256,1024]{2,1,0:T(8,128)(2,1)} %constant.110.clone.back_low_ref) | copy-start | bytes 12582916
  98.4 1.6 %copy-start.5 = (bf16[8,512,256]{2,1,0:T(8,128)(2,1)S(1)}, bf16[8,512,256]{2,1,0:T(8,128)(2,1)}, u32[]{:S(2)}) copy-start(bf16[8,512,256]{2,1,0:T(8,128)(2,1)} %constant.108.clone.low_ref) | copy-start | bytes 6291460
  116.1 14.7 %all-to-all-start.2 = ((f32[32,8,256]{2,1,0:T(8,128)}), f32[32,8,256]{2,1,0:T(8,128)S(1)}, u32[]{:S(2)}, u32[]{:S(2)}) async-start(f32[32,8,256]{2,1,0:T(8,128)} %correlate.1), calls=%async_computation.2 | async-start | bytes 524288 | tf_op jit(solution)/shard_map/all_to_all | solution.py:380

commit v2 on v1

--- a/solution.py
+++ b/solution.py
@@ -111,19 +111,105 @@
     return out
 
 
-def whiten_kernel(groups, series_ref, table_ref, taper_ref, white_ref, y_ref, spec_ref, pre_ref, suf_ref, all_ref):
+def own_index():
+    return lax.axis_index("blk") * lax.axis_size("lag") + lax.axis_index("lag")
+
+
+def coordinates(device):
+    n_lag = lax.axis_size("lag")
+    return (device // n_lag, device % n_lag)
+
+
+def greet_all(n_dev):
+    barrier = pltpu.get_barrier_semaphore()
+    me = own_index()
+
+    @pl.loop(1, n_dev)
+    def _(ahead):
+        other = (me + ahead) % n_dev
+        pl.semaphore_signal(barrier, inc=1, device_id=coordinates(other), device_id_type=pl.DeviceIdType.MESH)
+
+
+def meet_all(n_dev):
+    pl.semaphore_wait(pltpu.get_barrier_semaphore(), n_dev - 1)
+
+
+def slot_copy(src_ref, dst_ref, src, dst, send_sem, recv_sem, device):
+    return pltpu.make_async_remote_copy(
+        src_ref=src_ref.at[src],
+        dst_ref=dst_ref.at[dst],
+        send_sem=send_sem.at[src],
+        recv_sem=recv_sem.at[dst],
+        device_id=coordinates(device),
+        device_id_type=pl.DeviceIdType.MESH,
+    )
+
+
+def start_all(n_dev, src_ref, dst_ref, send_sem, recv_sem):
+    me = own_index()
+
+    @pl.loop(1, n_dev)
+    def _(ahead):
+        other = (me + ahead) % n_dev
+        slot_copy(src_ref, dst_ref, other, me, send_sem, recv_sem, other).start()
+
+
+def wait_all(n_dev, src_ref, dst_ref, send_sem, recv_sem):
+    me = own_index()
+
+    @pl.loop(1, n_dev)
+    def _(ahead):
+        other = (me + ahead) % n_dev
+        copy = slot_copy(src_ref, dst_ref, other, other, send_sem, recv_sem, other)
+        copy.wait_send()
+        copy.wait_recv()
+
+
+def whiten_kernel(
+    groups,
+    raw_ref,
+    table_ref,
+    taper_ref,
+    white_ref,
+    cast_ref,
+    series_ref,
+    ready_ref,
+    y_ref,
+    spec_ref,
+    pre_ref,
+    suf_ref,
+    all_ref,
+    raw_send,
+    raw_recv,
+    white_send,
+    white_recv,
+    own_sem,
+):
     step = pl.program_id(0)
     half = RADIX // 2
     rows = 16
+    n_dev, samples, chans = series_ref.shape
+    me = own_index()
 
     @pl.when(step == 0)
     def _():
+        greet_all(n_dev)
+        for other in range(n_dev):
+            cast_ref[other] = raw_ref[:, other * chans : (other + 1) * chans].astype(jnp.bfloat16)
+        meet_all(n_dev)
+        start_all(n_dev, cast_ref, series_ref, raw_send, raw_recv)
+        series_ref[me] = cast_ref[me]
+        wait_all(n_dev, cast_ref, series_ref, raw_send, raw_recv)
+        pieces = SPAN // samples
+        per_piece = samples // rows
+
         @pl.loop(0, SPAN // rows)
         def _(i):
             start = pl.multiple_of(i * rows, rows)
+            piece = i // per_piece
+            inside = pl.multiple_of((i % per_piece) * rows, rows)
             x = [
-                series_ref[pl.ds(pl.multiple_of(h * SPAN + start, rows), rows), :].astype(jnp.float32)
-                for h in range(RADIX)
+                series_ref[h * pieces + piece, pl.ds(inside, rows), :].astype(jnp.float32) for h in range(RADIX)
             ]
             y = real_dft16(x)
             y[0] = (y[0], y[half])
@@ -140,7 +226,6 @@
 
     @pl.when(step == half - 1)
     def _():
-        chans = series_ref.shape[1]
         edge = jnp.zeros((PAD, chans), jnp.float32)
         inner = pl.ds(PAD, M_ROWS)
 
@@ -167,17 +252,32 @@
             + pre_ref[last, pl.ds(PAD + 1, M_ROWS), :]
         )
         per = M_ROWS // groups
-        for rho in range(RADIX):
+
+        @pl.loop(0, RADIX)
+        def _(i):
+            rho = (me // groups + 1 + i) % RADIX
             total = all_ref[...] + suf_ref[rho, pl.ds(PAD - 2, M_ROWS), :] + pre_ref[rho, pl.ds(PAD + 2, M_ROWS), :]
             scale = taper_ref[rho] / (total / (2 * SW + 1) + EPS)
             for part in range(2):
                 value = (spec_ref[rho, pl.ds(part * M_ROWS, M_ROWS), :] * scale).astype(jnp.bfloat16)
                 for g in range(groups):
-                    white_ref[rho * groups + g, part] = value[g * per : (g + 1) * per]
-
-
-def whiten(series, n_dev):
-    chans = series.shape[1]
+                    ready_ref[rho * groups + g, part] = value[g * per : (g + 1) * per]
+            for g in range(groups):
+                other = rho * groups + g
+
+                @pl.when(other != me)
+                def _():
+                    slot_copy(ready_ref, white_ref, other, me, white_send, white_recv, other).start()
+
+        own = pltpu.make_async_copy(ready_ref.at[me], white_ref.at[me], own_sem)
+        own.start()
+        own.wait()
+        wait_all(n_dev, ready_ref, white_ref, white_send, white_recv)
+
+
+def whiten(raw, n_dev):
+    samples = raw.shape[0]
+    chans = C // n_dev
     groups = n_dev // RADIX
     half = RADIX // 2
     out = jax.ShapeDtypeStruct((n_dev, 2, M_ROWS // groups, chans), jnp.bfloat16)
@@ -186,22 +286,32 @@
         grid=(half,),
         out_shape=out,
         in_specs=[
-            pl.BlockSpec(series.shape, lambda i: (0, 0)),
+            pl.BlockSpec(raw.shape, lambda i: (0, 0)),
             pl.BlockSpec((1, 4 * M_ROWS, 2 * SPAN), lambda i: (i, 0, 0)),
             pl.BlockSpec((RADIX, M_ROWS, 1), lambda i: (0, 0, 0)),
         ],
-        out_specs=pl.BlockSpec(out.shape, lambda i: (0, 0, 0, 0)),
+        out_specs=pl.BlockSpec(memory_space=pl.ANY),
         scratch_shapes=[
+            pltpu.VMEM((n_dev, samples, chans), jnp.bfloat16),
+            pltpu.VMEM((n_dev, samples, chans), jnp.bfloat16),
+            pltpu.VMEM(out.shape, jnp.bfloat16),
             pltpu.VMEM((half, 2 * SPAN, chans), jnp.bfloat16),
             pltpu.VMEM((RADIX, 2 * M_ROWS, chans), jnp.float32),
             pltpu.VMEM((RADIX, M_ROWS + 2 * PAD, chans), jnp.float32),
             pltpu.VMEM((RADIX, M_ROWS + 2 * PAD, chans), jnp.float32),
             pltpu.VMEM((M_ROWS, chans), jnp.float32),
+            pltpu.SemaphoreType.DMA((n_dev,)),
+            pltpu.SemaphoreType.DMA((n_dev,)),
+            pltpu.SemaphoreType.DMA((n_dev,)),
+            pltpu.SemaphoreType.DMA((n_dev,)),
+            pltpu.SemaphoreType.DMA(()),
         ],
-        compiler_params=pltpu.CompilerParams(vmem_limit_bytes=40 * 2**20),
+        compiler_params=pltpu.CompilerParams(
+            vmem_limit_bytes=56 * 2**20, collective_id=0, has_side_effects=True
+        ),
         cost_estimate=pl.CostEstimate(flops=2 * 8 * 512 * 1024 * chans, bytes_accessed=12 * 2**20, transcendentals=0),
         name="whiten",
-    )(series, jnp.asarray(spectrum_tables()), jnp.asarray(taper_table()))
+    )(raw, jnp.asarray(spectrum_tables()), jnp.asarray(taper_table()))
 
 
 def split_rounded(value):
@@ -210,7 +320,24 @@
 
 
 def correlate_kernel(
-    blocks, mask_ref, white_ref, waves_ref, high_ref, low_ref, back_high_ref, back_low_ref, out_ref, lhs_ref, re_ref, im_ref, h_ref, acc_ref
+    blocks,
+    mask_ref,
+    white_ref,
+    waves_ref,
+    high_ref,
+    low_ref,
+    back_high_ref,
+    back_low_ref,
+    out_ref,
+    lhs_ref,
+    re_ref,
+    im_ref,
+    h_ref,
+    acc_ref,
+    part_ref,
+    got_ref,
+    send_sem,
+    recv_sem,
 ):
     step = pl.program_id(0)
     sources, _, bins, chans = white_ref.shape
@@ -221,6 +348,7 @@
 
     @pl.when(step == 0)
     def _():
+        greet_all(sources)
         acc_ref[...] = jnp.zeros_like(acc_ref)
         for s in range(sources):
             block, place = divmod(s, per_block)
@@ -281,7 +409,8 @@
 
     @pl.when(step == pl.num_programs(0) - 1)
     def _():
-        devices, _, cols = out_ref.shape
+        devices, _, cols = part_ref.shape
+        me = own_index()
         parts = width // cols
         for segment in range(2 * blocks):
             value = jnp.zeros((LAGS, width), f32)
@@ -290,7 +419,12 @@
             if segment > 0:
                 value = value + acc_ref[pl.ds((segment - 1) * LAGS, LAGS), pl.ds(width, width)]
             for part in range(parts):
-                out_ref[segment * parts + part] = value[:, part * cols : (part + 1) * cols]
+                part_ref[segment * parts + part] = value[:, part * cols : (part + 1) * cols]
+        meet_all(devices)
+        start_all(devices, part_ref, got_ref, send_sem, recv_sem)
+        got_ref[me] = part_ref[me]
+        wait_all(devices, part_ref, got_ref, send_sem, recv_sem)
+        out_ref[...] = jnp.sum(got_ref[...], axis=0)
 
 
 def correlate(white, mask, waves):
@@ -302,7 +436,8 @@
     high, low = channel_tables(width, chunk)
     back_high, back_low = offset_tables(width, chunk)
     rows = (2 * blocks - 1) * LAGS
-    out = jax.ShapeDtypeStruct((n_dev, LAGS, 2 * C // n_dev), jnp.float32)
+    cols = 2 * C // n_dev
+    out = jax.ShapeDtypeStruct((LAGS, cols), jnp.float32)
     table = pl.BlockSpec((1, width, 2 * chunk), lambda i: (i, 0, 0))
     back = pl.BlockSpec((1, 2 * chunk, size), lambda i: (i, 0, 0))
     return pl.pallas_call(
@@ -318,15 +453,21 @@
             back,
             back,
         ],
-        out_specs=pl.BlockSpec(out.shape, lambda i: (0, 0, 0)),
+        out_specs=pl.BlockSpec(out.shape, lambda i: (0, 0)),
         scratch_shapes=[
             pltpu.VMEM((blocks * 2 * bins, width), jnp.bfloat16),
             pltpu.VMEM((blocks, bins, chunk), jnp.float32),
             pltpu.VMEM((blocks, bins, chunk), jnp.float32),
             pltpu.VMEM((rows, 2 * chunk), jnp.float32),
             pltpu.VMEM((rows, size), jnp.float32),
+            pltpu.VMEM((n_dev, LAGS, cols), jnp.float32),
+            pltpu.VMEM((n_dev, LAGS, cols), jnp.float32),
+            pltpu.SemaphoreType.DMA((n_dev,)),
+            pltpu.SemaphoreType.DMA((n_dev,)),
         ],
-        compiler_params=pltpu.CompilerParams(vmem_limit_bytes=40 * 2**20),
+        compiler_params=pltpu.CompilerParams(
+            vmem_limit_bytes=56 * 2**20, collective_id=1, has_side_effects=True
+        ),
         cost_estimate=pl.CostEstimate(flops=5 * 2**30, bytes_accessed=14 * 2**20, transcendentals=0),
         name="correlate",
     )(
@@ -369,16 +510,11 @@
 
 
 def on_device(raw, mask):
-    axes = ("blk", "lag")
     n_dev = lax.axis_size("blk") * lax.axis_size("lag")
-    device = lax.axis_index("blk") * lax.axis_size("lag") + lax.axis_index("lag")
-    series = lax.all_to_all(raw.astype(jnp.bfloat16), axes, split_axis=1, concat_axis=0, tiled=True)
-    white = whiten(series, n_dev)
+    device = own_index()
+    white = whiten(raw, n_dev)
     waves = lag_waves(device, white.shape[2], n_dev // RADIX)
-    white = lax.all_to_all(white, axes, split_axis=0, concat_axis=0, tiled=True)
-    partial = correlate(white, mask, waves)
-    shares = lax.all_to_all(partial, axes, split_axis=0, concat_axis=0, tiled=True)
-    total = jnp.sum(shares, axis=0)
+    total = correlate(white, mask, waves)
     n_cols = total.shape[1]
     counts = pair_counts(mask, device * n_cols + lax.iota(jnp.int32, n_cols))
     return total * stack_scale(counts)[None, :]

time: 132 us -> 120 us (0.909)
  Pallas kernels: 22.9 us -> 116 us
  blocking collectives: 54.6 us -> 0 us
  waiting for transfers between devices: 34.8 us -> 0 us
  starting transfers between devices: 8.92 us -> 0 us
  local copies, waits for them, and re-layouts: 6.1 us -> 0.86 us
  other arithmetic: 3.86 us -> 2.27 us
    pallas_call x1, Pallas kernels: 6.82 us -> 89 us  [whiten(): pl.pallas_call(functools.partial(whiten_kernel, groups), grid=(half,), ou...]
    all_to_all x1 -> x0, blocking collectives: 54.6 us -> none  [on_device(): lax.all_to_all(raw.astype(jnp.bfloat16), axes, split_axis=1, concat_axis=...]
    all_to_all x2 -> x0, waiting for transfers between devices: 34.8 us -> none  [the longest x1 24.8 us: on_device(): white = lax.all_to_all(white, axes, split_axis=0, concat_axis=0, tiled=True)]
    pallas_call x1, Pallas kernels: 16.1 us -> 27.2 us  [correlate(): pl.pallas_call(functools.partial(correlate_kernel, blocks), grid=(size //...]
    all_to_all x2 -> x0, starting transfers between devices: 8.92 us -> none  [the longest x1 4.46 us: on_device(): lax.all_to_all(partial, axes, split_axis=0, concat_axis=0, tiled=True)]
    unnamed x14 -> x2, local copies, waits for them, and re-layouts: 5.98 us -> 0.01 us
    all_to_all x1 -> x0, other arithmetic: 2.84 us -> none  [on_device(): lax.all_to_all(raw.astype(jnp.bfloat16), axes, split_axis=1, concat_axis=...]
  transfers between devices with their start and end apart: 2 -> 0, of which waited for: 2 -> 0; matrix products, arithmetic and copies ran while one was open for 0% -> 0% of each run, Pallas kernels for 0% -> 0%
where the time goes in v2:
time: 120 us; the launch traced here: 119 us
  Pallas kernels  116 us (97%)
  other arithmetic  2.27 us (2%)
    pallas_call x1, Pallas kernels, whiten(): pl.pallas_call(functools.partial(whiten_kernel, groups), grid=(half,), ou...  89 us
    pallas_call x1, Pallas kernels, correlate(): pl.pallas_call(functools.partial(correlate_kernel, blocks), grid=(size //...  27.2 us

profile of v2, /device:TPU:0, one launch (start us, length us, event | category | flops | bytes accessed | tf_op | source)
XLA Modules:
  0.0 119.4 jit_solution(12050034707904358155)
XLA Ops:
  0.0 0.1 fusion.4
  0.2 0.9 broadcast_in_dim.2.waves_ref
  1.0 0.0 copy-start
  1.0 89.0 %whiten.1.white_ref = bf16[32,2,64,128]{3,2,1,0:T(8,128)(2,1)} custom-call(f32[256,4096]{1,0:T(8,128)} %raw_ref.1, bf16[8,512,1024]{2,1,0:T(8,128)(2,1)} %constant.103.clone.table_ref, f32[16,128,1]{2,1,0:T(8,128)} %constant.104.clone.taper_ref), custom_call_target="tpu_custom_call" | custom-call | flops 1073741824 | bytes 12582912 | tf_op jit(solution)/shard_map/whiten/pallas_call | solution.py:284
  90.0 0.0 copy-done
  90.0 0.6 convert_element_type.14.mask_ref
  90.6 27.2 %correlate.1 = f32[8,256]{1,0:T(8,128)} custom-call(f32[8,8]{1,0:T(8,128)} %convert_element_type.14.mask_ref, bf16[32,2,64,128]{3,2,1,0:T(8,128)(2,1)} %whiten.1.white_ref, f32[8,64,128]{2,1,0:T(8,128)} %broadcast_in_dim.2.waves_ref, bf16[8,512,256]{2,1,0:T(8,128)(2,1)} %constant.105.clone.high_ref, bf16[8,512,256]{2,1,0:T(8,128)(2,1)} %constant.106.clone.low_ref, ...), custom_call_target="tpu_custom_call" | custom-call | flops 5368709120 | bytes 14680064 | tf_op jit(solution)/shard_map/correlate/pallas_call | solution.py:443
  117.9 0.1 select_reduce_fusion
  118.0 0.1 multiply_reduce_fusion
  118.1 1.3 %broadcast_multiply_fusion = f32[8,256]{1,0:T(8,128)} fusion(f32[8,256]{1,0:T(8,128)} %correlate.1, f32[256]{0:T(256)S(1)} %multiply_rsqrt_fusion), kind=kLoop, calls=%fused_computation.3 | loop fusion | flops 2048 | bytes 17408 | tf_op jit(solution)/shard_map/mul | solution.py:520
  (8 shorter events, 0.1 us)
Async XLA Ops:
  1.0 89.0 %copy-start = (s32[8,8]{1,0:T(8,128)S(1)}, s32[8,8]{1,0:T(8,128)}, u32[]{:S(2)}) copy-start(s32[8,8]{1,0:T(8,128)} %param.9) | copy-start | bytes 772

commit v3 on v1

v3 whole, which is shorter than its diff:
```python
import functools
import math

import jax
import jax.numpy as jnp
import ml_dtypes
import numpy as np
from jax import lax
from jax.experimental import pallas as pl
from jax.experimental.pallas import tpu as pltpu
from jax.sharding import PartitionSpec as P

NT = 8192
C = 4096
NB = 2048
K0 = 16
SW = 32
TAPER = 128
LAGS = 8
LAG_STEP = 32
EPS = 1e-06

RADIX = 16
RAW_CHUNKS = 4
BIN_CHUNK = 16
SPAN = NT // RADIX
M_ROWS = NB // RADIX
LANES = 128
PAD = 8
bf16 = ml_dtypes.bfloat16


def split_high_low(table):
    high = table.astype(bf16)
    low = (table - high.astype(np.float64)).astype(bf16)
    return high, low


@functools.cache
def spectrum_tables(samples):
    m = np.arange(M_ROWS)[:, None] + 1
    s = np.arange(SPAN)[None, :]

    def waves(rho):
        angle = 2 * np.pi * (((RADIX * m + rho) * s) % NT) / NT
        return np.cos(angle), np.sin(angle)

    zero = np.zeros((M_ROWS, SPAN))
    tables = []
    c0, s0 = waves(0)
    c8, s8 = waves(RADIX // 2)
    tables.append(np.block([[c0, zero], [-s0, zero], [zero, c8], [zero, -s8]]))
    for rho in range(1, RADIX // 2):
        ca, sa = waves(rho)
        cb, sb = waves(RADIX - rho)
        tables.append(np.block([[ca, sa], [-sa, ca], [cb, -sb], [-sb, -cb]]))
    table = np.stack(tables).astype(bf16)
    rows = samples // RAW_CHUNKS
    shape = (RADIX // 2, 4 * M_ROWS, 2, SPAN // samples, RAW_CHUNKS, rows)
    table = table.reshape(shape).transpose(4, 0, 1, 2, 3, 5)
    return table.reshape(RAW_CHUNKS, RADIX // 2, 4 * M_ROWS, 2 * SPAN // RAW_CHUNKS)


@functools.cache
def taper_table():
    j = np.arange(NB, dtype=np.float64)
    edge = np.minimum(j, NB - 1 - j)
    weights = np.where(edge < TAPER, 0.5 - 0.5 * np.cos(math.pi * (edge + 0.5) / TAPER), 1.0)
    weights = weights.reshape(M_ROWS, RADIX).T
    return np.ascontiguousarray(weights.astype(np.float32)[:, :, None])


@functools.cache
def channel_tables(width, chunk):
    size = 2 * width
    c = np.arange(width)[:, None]
    q = np.arange(size)[None, :]
    angle = 2 * np.pi * ((c * q) % size) / size
    both = np.stack([np.cos(angle), np.sin(angle)], axis=1).reshape(width, 2, size // chunk, chunk)
    both = both.transpose(2, 0, 1, 3).reshape(size // chunk, width, 2 * chunk)
    return split_high_low(both)


@functools.cache
def offset_tables(width, chunk):
    size = 2 * width
    q = np.arange(size)[:, None]
    d = np.arange(size)[None, :] - width
    angle = 2 * np.pi * ((q * d) % size) / size
    both = np.stack([np.cos(angle), np.sin(angle)]) / size
    both[:, :, 0] = 0.0
    both = both.reshape(2, size // chunk, chunk, size).transpose(1, 0, 2, 3)
    return split_high_low(both.reshape(size // chunk, 2 * chunk, size))


def real_dft16(x):
    a = [x[h] + x[h + 8] for h in range(8)]
    b = [x[h] - x[h + 8] for h in range(8)]
    out = {}
    lo = [a[h] + a[h + 4] for h in range(4)]
    d = [a[h] - a[h + 4] for h in range(4)]
    out[0] = (lo[0] + lo[2]) + (lo[1] + lo[3])
    out[8] = (lo[0] + lo[2]) - (lo[1] + lo[3])
    out[4] = (lo[0] - lo[2], lo[3] - lo[1])
    root = math.sqrt(0.5)
    minus, plus = (d[1] - d[3]) * root, (d[1] + d[3]) * root
    out[2] = (d[0] + minus, -(d[2] + plus))
    out[6] = (d[0] - minus, d[2] - plus)
    diff = [None] + [b[h] - b[8 - h] for h in range(1, 4)]
    add = [None] + [b[h] + b[8 - h] for h in range(1, 4)]
    for rho in (1, 3, 5, 7):
        re, im = b[0], b[4] * (-math.sin(math.pi * rho / 2))
        for h in range(1, 4):
            re = re + diff[h] * math.cos(math.pi * h * rho / 8)
            im = im - add[h] * math.sin(math.pi * h * rho / 8)
        out[rho] = (re, im)
    return out


def own_index():
    return lax.axis_index("blk") * lax.axis_size("lag") + lax.axis_index("lag")


def coordinates(device):
    n_lag = lax.axis_size("lag")
    return (device // n_lag, device % n_lag)


def greet_all(n_dev):
    barrier = pltpu.get_barrier_semaphore()
    me = own_index()

    @pl.loop(1, n_dev)
    def _(ahead):
        other = (me + ahead) % n_dev
        pl.semaphore_signal(barrier, inc=1, device_id=coordinates(other), device_id_type=pl.DeviceIdType.MESH)


def meet_all(n_dev):
    pl.semaphore_wait(pltpu.get_barrier_semaphore(), n_dev - 1)


def split_rounded(value):
    high = value.astype(jnp.bfloat16)
    return high, (value - high.astype(jnp.float32)).astype(jnp.bfloat16)


def slot_copy(src_ref, dst_ref, chunk, src, dst, send_sem, recv_sem, device):
    return pltpu.make_async_remote_copy(
        src_ref=src_ref.at[chunk, src],
        dst_ref=dst_ref.at[chunk, dst],
        send_sem=send_sem.at[chunk, src],
        recv_sem=recv_sem.at[chunk, dst],
        device_id=coordinates(device),
        device_id_type=pl.DeviceIdType.MESH,
    )


def start_all(n_dev, chunk, src_ref, dst_ref, send_sem, recv_sem):
    me = own_index()

    @pl.loop(1, n_dev)
    def _(ahead):
        other = (me + ahead) % n_dev
        slot_copy(src_ref, dst_ref, chunk, other, me, send_sem, recv_sem, other).start()


def wait_all(n_dev, chunk, src_ref, dst_ref, send_sem, recv_sem):
    me = own_index()

    @pl.loop(1, n_dev)
    def _(ahead):
        other = (me + ahead) % n_dev
        copy = slot_copy(src_ref, dst_ref, chunk, other, other, send_sem, recv_sem, other)
        copy.wait_send()
        copy.wait_recv()


def transform(series_ref, chunk, y_ref, spec_ref, table_ref):
    half = RADIX // 2
    tile = 16
    _, n_dev, rows, _ = series_ref.shape
    pieces = n_dev // RADIX
    span = pieces * rows
    per_piece = rows // tile

    @pl.loop(0, span // tile)
    def _(i):
        start = pl.multiple_of(i * tile, tile)
        inside = pl.multiple_of((i % per_piece) * tile, tile)
        x = [
            series_ref[chunk, h * pieces + i // per_piece, pl.ds(inside, tile), :].astype(jnp.float32)
            for h in range(RADIX)
        ]
        y = real_dft16(x)
        y[0] = (y[0], y[half])
        for rho in range(half):
            for part in range(2):
                y_ref[rho, pl.ds(part * span + start, tile), :] = y[rho][part].astype(jnp.bfloat16)

    @pl.loop(0, half)
    def _(pair):
        both = jnp.dot(table_ref[chunk, pair], y_ref[pair], preferred_element_type=jnp.float32)
        other = jnp.where(pair == 0, half, RADIX - pair)
        spec_ref[pair] += both[: 2 * M_ROWS]
        spec_ref[other] += both[2 * M_ROWS :]


def window_sums(spec_ref, pre_ref, suf_ref, all_ref):
    edge = jnp.zeros((PAD, all_ref.shape[1]), jnp.float32)
    inner = pl.ds(PAD, M_ROWS)
    for rho in range(RADIX):
        re = spec_ref[rho, pl.ds(0, M_ROWS), :]
        im = spec_ref[rho, pl.ds(M_ROWS, M_ROWS), :]
        amp = jnp.sqrt(re * re + im * im)
        suf_ref[rho, inner, :] = amp
        pre_ref[rho, inner, :] = amp if rho == 0 else pre_ref[rho - 1, inner, :] + amp
        for ref in (pre_ref, suf_ref):
            ref[rho, pl.ds(0, PAD), :] = edge
            ref[rho, pl.ds(PAD + M_ROWS, PAD), :] = edge
    for rho in range(RADIX - 2, -1, -1):
        suf_ref[rho, inner, :] = suf_ref[rho, inner, :] + suf_ref[rho + 1, inner, :]
    last = RADIX - 1
    all_ref[...] = (
        pre_ref[last, pl.ds(PAD - 1, M_ROWS), :]
        + pre_ref[last, inner, :]
        + pre_ref[last, pl.ds(PAD + 1, M_ROWS), :]
    )


def cross_spectra(blocks, bin_chunk, q, mask_ref, waves_ref, lhs_ref, high_ref, low_ref, re_ref, im_ref, sums_ref):
    f32 = jnp.float32
    half = LAGS // 2
    chunk = re_ref.shape[2]
    bins = BIN_CHUNK
    lhs = lhs_ref[...]
    product = jnp.dot(lhs, high_ref[q], preferred_element_type=f32)
    product = product + jnp.dot(lhs, low_ref[q], preferred_element_type=f32)
    for block in range(blocks):
        real = product[2 * block * bins : (2 * block + 1) * bins]
        imag = product[(2 * block + 1) * bins : (2 * block + 2) * bins]
        re_ref[block] = real[:, :chunk] + imag[:, chunk:]
        im_ref[block] = imag[:, :chunk] - real[:, chunk:]
    for delta in range(blocks):
        sums = [sums_ref[q, delta * 4 * half + n] for n in range(4 * half)]
        for b in range(bins // 8):
            rows = pl.ds(8 * b, 8)
            wave_rows = pl.ds(pl.multiple_of(bin_chunk * bins + 8 * b, 8), 8)
            g_re = jnp.zeros((8, chunk), f32)
            g_im = jnp.zeros((8, chunk), f32)
            for block in range(blocks - delta):
                keep = mask_ref[block, block + delta]
                a_re, a_im = re_ref[block, rows, :], im_ref[block, rows, :]
                if delta == 0:
                    g_re = g_re + keep * (a_re * a_re + a_im * a_im)
                else:
                    b_re, b_im = re_ref[block + delta, rows, :], im_ref[block + delta, rows, :]
                    g_re = g_re + keep * (a_re * b_re + a_im * b_im)
                    g_im = g_im + keep * (a_im * b_re - a_re * b_im)
            for j in range(half):
                cosine, sine = waves_ref[j, wave_rows, :], waves_ref[half + j, wave_rows, :]
                sums[4 * j] = sums[4 * j] + cosine * g_re
                sums[4 * j + 1] = sums[4 * j + 1] + sine * g_re
                if delta > 0:
                    sums[4 * j + 2] = sums[4 * j + 2] + cosine * g_im
                    sums[4 * j + 3] = sums[4 * j + 3] + sine * g_im
        for n in range(4 * half):
            sums_ref[q, delta * 4 * half + n] = sums[n]


def to_offsets(blocks, q, sums_ref, h_ref, back_high_ref, back_low_ref, acc_ref):
    f32 = jnp.float32
    half = LAGS // 2
    chunk = sums_ref.shape[3]
    zero_row = (blocks - 1) * LAGS
    for delta in range(blocks):
        h_re, h_im = [None] * LAGS, [None] * LAGS
        for j in range(half):
            cr, sr, ci, si = [
                jnp.sum(sums_ref[q, (delta * half + j) * 4 + n], axis=0, keepdims=True) for n in range(4)
            ]
            h_re[half + j], h_im[half + j] = cr - si, ci + sr
            h_re[half - 1 - j], h_im[half - 1 - j] = cr + si, ci - sr
        ahead = zero_row + delta * LAGS
        h_ref[pl.ds(ahead, LAGS), pl.ds(0, chunk)] = jnp.concatenate(h_re, axis=0)
        h_ref[pl.ds(ahead, LAGS), pl.ds(chunk, chunk)] = jnp.concatenate(h_im, axis=0)
        if delta > 0:
            behind = zero_row - delta * LAGS
            h_ref[pl.ds(behind, LAGS), pl.ds(0, chunk)] = jnp.concatenate(h_re[::-1], axis=0)
            h_ref[pl.ds(behind, LAGS), pl.ds(chunk, chunk)] = -jnp.concatenate(h_im[::-1], axis=0)
    h_high, h_low = split_rounded(h_ref[...])
    acc_ref[...] += (
        jnp.dot(h_high, back_high_ref[q], preferred_element_type=f32)
        + jnp.dot(h_low, back_high_ref[q], preferred_element_type=f32)
        + jnp.dot(h_high, back_low_ref[q], preferred_element_type=f32)
    )


def stack_kernel(
    blocks,
    mask_ref,
    waves_ref,
    taper_ref,
    raw_hbm,
    table_hbm,
    high_hbm,
    low_hbm,
    back_high_hbm,
    back_low_hbm,
    out_ref,
    raw_ref,
    table_ref,
    high_ref,
    low_ref,
    back_high_ref,
    back_low_ref,
    cast_ref,
    series_ref,
    y_ref,
    spec_ref,
    pre_ref,
    suf_ref,
    all_ref,
    ready_ref,
    white_ref,
    lhs_ref,
    re_ref,
    im_ref,
    sums_ref,
    h_ref,
    acc_ref,
    part_ref,
    got_ref,
    raw_sem,
    table_sem,
    raw_send,
    raw_recv,
    white_send,
    white_recv,
    stack_send,
    stack_recv,
):
    _, n_dev, rows, chans = series_ref.shape
    groups = n_dev // RADIX
    me = own_index()
    f32 = jnp.float32

    def raw_copy(chunk):
        part = pl.ds(pl.multiple_of(chunk * rows, rows), rows)
        return pltpu.make_async_copy(raw_hbm.at[part], raw_ref.at[part], raw_sem.at[chunk])

    def table_copy(n):
        pairs = (
            (table_hbm, table_ref),
            (high_hbm, high_ref),
            (low_hbm, low_ref),
            (back_high_hbm, back_high_ref),
            (back_low_hbm, back_low_ref),
        )
        src, dst = pairs[n]
        return pltpu.make_async_copy(src, dst, table_sem.at[n])

    n_tables = 5

    for chunk in range(RAW_CHUNKS):
        raw_copy(chunk).start()
    greet_all(n_dev)

    def send_raw(chunk):
        part = pl.ds(pl.multiple_of(chunk * rows, rows), rows)
        raw_copy(chunk).wait()
        for other in range(n_dev):
            cast_ref[chunk, other] = raw_ref[part, other * chans : (other + 1) * chans].astype(jnp.bfloat16)

    send_raw(0)
    meet_all(n_dev)
    start_all(n_dev, 0, cast_ref, series_ref, raw_send, raw_recv)

    @pl.loop(1, RAW_CHUNKS)
    def _(chunk):
        send_raw(chunk)
        start_all(n_dev, chunk, cast_ref, series_ref, raw_send, raw_recv)

    for n in range(n_tables):
        table_copy(n).start()
    spec_ref[...] = jnp.zeros_like(spec_ref)
    sums_ref[...] = jnp.zeros_like(sums_ref)
    acc_ref[...] = jnp.zeros_like(acc_ref)
    table_copy(0).wait()

    @pl.loop(0, RAW_CHUNKS)
    def _(chunk):
        series_ref[chunk, me] = cast_ref[chunk, me]
        wait_all(n_dev, chunk, cast_ref, series_ref, raw_send, raw_recv)
        transform(series_ref, chunk, y_ref, spec_ref, table_ref)

    window_sums(spec_ref, pre_ref, suf_ref, all_ref)
    bin_chunks = ready_ref.shape[0]
    per = bin_chunks * BIN_CHUNK

    @pl.loop(0, RADIX)
    def _(i):
        rho = (me // groups + 1 + i) % RADIX
        total = all_ref[...] + suf_ref[rho, pl.ds(PAD - 2, M_ROWS), :] + pre_ref[rho, pl.ds(PAD + 2, M_ROWS), :]
        scale = taper_ref[rho] / (total / (2 * SW + 1) + EPS)
        for part in range(2):
            value = (spec_ref[rho, pl.ds(part * M_ROWS, M_ROWS), :] * scale).astype(jnp.bfloat16)
            for g in range(groups):
                for w in range(bin_chunks):
                    first = g * per + w * BIN_CHUNK
                    ready_ref[w, rho * groups + g, part] = value[first : first + BIN_CHUNK]
        for g in range(groups):
            other = rho * groups + g

            @pl.when(other != me)
            def _():
                slot_copy(ready_ref, white_ref, 0, other, me, white_send, white_recv, other).start()

    @pl.loop(1, bin_chunks)
    def _(w):
        start_all(n_dev, w, ready_ref, white_ref, white_send, white_recv)

    for n in range(1, n_tables):
        table_copy(n).wait()
    per_block = n_dev // blocks
    q_chunks = sums_ref.shape[0]

    @pl.loop(0, bin_chunks)
    def _(w):
        white_ref[w, me] = ready_ref[w, me]
        wait_all(n_dev, w, ready_ref, white_ref, white_send, white_recv)
        for source in range(n_dev):
            block, place = divmod(source, per_block)
            for part in range(2):
                lhs_ref[pl.ds((2 * block + part) * BIN_CHUNK, BIN_CHUNK), pl.ds(place * chans, chans)] = white_ref[
                    w, source, part
                ]

        @pl.loop(0, q_chunks)
        def _(q):
            cross_spectra(
                blocks, w, q, mask_ref, waves_ref, lhs_ref, high_ref, low_ref, re_ref, im_ref, sums_ref
            )

    @pl.loop(0, q_chunks)
    def _(q):
        to_offsets(blocks, q, sums_ref, h_ref, back_high_ref, back_low_ref, acc_ref)

    width = per_block * chans
    cols = part_ref.shape[3]
    parts = width // cols
    for segment in range(2 * blocks):
        value = jnp.zeros((LAGS, width), f32)
        if segment < 2 * blocks - 1:
            value = value + acc_ref[pl.ds(segment * LAGS, LAGS), pl.ds(0, width)]
        if segment > 0:
            value = value + acc_ref[pl.ds((segment - 1) * LAGS, LAGS), pl.ds(width, width)]
        for part in range(parts):
            part_ref[0, segment * parts + part] = value[:, part * cols : (part + 1) * cols]
    start_all(n_dev, 0, part_ref, got_ref, stack_send, stack_recv)
    got_ref[0, me] = part_ref[0, me]
    wait_all(n_dev, 0, part_ref, got_ref, stack_send, stack_recv)
    out_ref[...] = jnp.sum(got_ref[0], axis=0)


def stacked(raw, mask, waves, n_dev):
    samples = raw.shape[0]
    chans = C // n_dev
    blocks = mask.shape[0]
    bins = NB // n_dev
    width = C // blocks
    size = 2 * width
    chunk = LANES
    cols = 2 * C // n_dev
    bin_chunks = bins // BIN_CHUNK
    pairs = RADIX // 2
    f32, b16 = jnp.float32, jnp.bfloat16
    tables = [spectrum_tables(samples), *channel_tables(width, chunk), *offset_tables(width, chunk)]
    rows = (2 * blocks - 1) * LAGS
    whole = pl.BlockSpec(memory_space=pltpu.VMEM)
    away = pl.BlockSpec(memory_space=pl.ANY)
    return pl.pallas_call(
        functools.partial(stack_kernel, blocks),
        out_shape=jax.ShapeDtypeStruct((LAGS, cols), f32),
        in_specs=[pl.BlockSpec(memory_space=pltpu.SMEM), whole, whole] + [away] * 6,
        out_specs=whole,
        scratch_shapes=[
            pltpu.VMEM(raw.shape, f32),
            *[pltpu.VMEM(table.shape, b16) for table in tables],
            pltpu.VMEM((RAW_CHUNKS, n_dev, samples // RAW_CHUNKS, chans), b16),
            pltpu.VMEM((RAW_CHUNKS, n_dev, samples // RAW_CHUNKS, chans), b16),
            pltpu.VMEM((pairs, 2 * SPAN // RAW_CHUNKS, chans), b16),
            pltpu.VMEM((RADIX, 2 * M_ROWS, chans), f32),
            pltpu.VMEM((RADIX, M_ROWS + 2 * PAD, chans), f32),
            pltpu.VMEM((RADIX, M_ROWS + 2 * PAD, chans), f32),
            pltpu.VMEM((M_ROWS, chans), f32),
            pltpu.VMEM((bin_chunks, n_dev, 2, BIN_CHUNK, chans), b16),
            pltpu.VMEM((bin_chunks, n_dev, 2, BIN_CHUNK, chans), b16),
            pltpu.VMEM((blocks * 2 * BIN_CHUNK, width), b16),
            pltpu.VMEM((blocks, BIN_CHUNK, chunk), f32),
            pltpu.VMEM((blocks, BIN_CHUNK, chunk), f32),
            pltpu.VMEM((size // chunk, blocks * 2 * LAGS, 8, chunk), f32),
            pltpu.VMEM((rows, 2 * chunk), f32),
            pltpu.VMEM((rows, size), f32),
            pltpu.VMEM((1, n_dev, LAGS, cols), f32),
            pltpu.VMEM((1, n_dev, LAGS, cols), f32),
            pltpu.SemaphoreType.DMA((RAW_CHUNKS,)),
            pltpu.SemaphoreType.DMA((len(tables),)),
            pltpu.SemaphoreType.DMA((RAW_CHUNKS, n_dev)),
            pltpu.SemaphoreType.DMA((RAW_CHUNKS, n_dev)),
            pltpu.SemaphoreType.DMA((bin_chunks, n_dev)),
            pltpu.SemaphoreType.DMA((bin_chunks, n_dev)),
            pltpu.SemaphoreType.DMA((1, n_dev)),
            pltpu.SemaphoreType.DMA((1, n_dev)),
        ],
        compiler_params=pltpu.CompilerParams(
            vmem_limit_bytes=58 * 2**20, collective_id=0, has_side_effects=True
        ),
        cost_estimate=pl.CostEstimate(flops=6 * 2**30, bytes_accessed=25 * 2**20, transcendentals=0),
        name="stacked",
    )(mask.astype(f32), waves, jnp.asarray(taper_table()), raw, *[jnp.asarray(table) for table in tables])


def lag_waves(device, bins, groups):
    rho, group = device // groups, device % groups
    k = RADIX * (group * bins + lax.iota(jnp.int32, bins) + 1) + rho
    number = lax.iota(jnp.int32, LAGS // 2) + LAGS // 2
    shifts = LAG_STEP * (2 * number + 1 - LAGS) // 2
    phase = jnp.mod(shifts[:, None] * k[None, :], NT).astype(jnp.float32) * (2 * math.pi / NT)
    waves = jnp.concatenate([jnp.cos(phase), jnp.sin(phase)], axis=0)
    return jnp.broadcast_to(waves[:, :, None], (LAGS, bins, LANES))


def pair_counts(mask, columns):
    blocks = mask.shape[0]
    width = C // blocks
    labels = lax.iota(jnp.int32, blocks)
    apart = labels[None, :] - labels[:, None]
    deltas = lax.iota(jnp.int32, 2 * blocks - 1) - (blocks - 1)
    per_delta = jnp.sum(
        mask[None] * (apart[None] == deltas[:, None, None]).astype(jnp.int32), axis=(1, 2)
    )
    offsets = columns - C
    intersection = jnp.maximum(0, width - jnp.abs(offsets[:, None] - width * deltas[None, :]))
    return jnp.sum(intersection * per_delta[None, :], axis=1)


def stack_scale(counts):
    return 1.0 / jnp.sqrt(NB * jnp.maximum(counts, 1).astype(jnp.float32))


def on_device(raw, mask):
    n_dev = lax.axis_size("blk") * lax.axis_size("lag")
    device = own_index()
    waves = lag_waves(device, NB // n_dev, n_dev // RADIX)
    total = stacked(raw, mask, waves, n_dev)
    n_cols = total.shape[1]
    counts = pair_counts(mask, device * n_cols + lax.iota(jnp.int32, n_cols))
    return total * stack_scale(counts)[None, :]


def solution(mesh):
    return jax.shard_map(
        on_device,
        mesh=mesh,
        in_specs=(P(("blk", "lag"), None), P()),
        out_specs=P(None, ("blk", "lag")),
        check_vma=False,
    )
```

time: 132 us -> 110 us (0.83)
  Pallas kernels: 22.9 us -> 106 us
  blocking collectives: 54.6 us -> 0 us
  waiting for transfers between devices: 34.8 us -> 0 us
  starting transfers between devices: 8.92 us -> 0 us
  local copies, waits for them, and re-layouts: 6.1 us -> 0.83 us
    pallas_call x2 -> x1, Pallas kernels: 22.9 us -> 106 us  [stacked(): pl.pallas_call(functools.partial(stack_kernel, blocks), out_shape=jax.Sha...]
    all_to_all x1 -> x0, blocking collectives: 54.6 us -> none  [on_device(): lax.all_to_all(raw.astype(jnp.bfloat16), axes, split_axis=1, concat_axis=...]
    all_to_all x2 -> x0, waiting for transfers between devices: 34.8 us -> none  [the longest x1 24.8 us: on_device(): white = lax.all_to_all(white, axes, split_axis=0, concat_axis=0, tiled=True)]
    all_to_all x2 -> x0, starting transfers between devices: 8.92 us -> none  [the longest x1 4.46 us: on_device(): lax.all_to_all(partial, axes, split_axis=0, concat_axis=0, tiled=True)]
    unnamed x14 -> x2, local copies, waits for them, and re-layouts: 5.98 us -> 0.01 us
    all_to_all x1 -> x0, other arithmetic: 2.84 us -> none  [on_device(): lax.all_to_all(raw.astype(jnp.bfloat16), axes, split_axis=1, concat_axis=...]
  transfers between devices with their start and end apart: 2 -> 0, of which waited for: 2 -> 0; matrix products, arithmetic and copies ran while one was open for 0% -> 0% of each run, Pallas kernels for 0% -> 0%
where the time goes in v3:
time: 110 us
  Pallas kernels  106 us (96%)
  other arithmetic  2.95 us (3%)
    pallas_call x1, Pallas kernels, stacked(): pl.pallas_call(functools.partial(stack_kernel, blocks), out_shape=jax.Sha...  106 us

profile of v3, /device:TPU:0, one launch (start us, length us, event | category | flops | bytes accessed | tf_op | source)
XLA Modules:
  0.0 109.9 jit_solution(9821114225360347951)
XLA Ops:
  0.0 0.1 fusion.4
  0.2 0.8 broadcast_in_dim.2.waves_ref
  1.0 1.3 %convert_element_type.14.mask_ref = f32[8,8]{1,0:T(8,128)} convert(s32[8,8]{1,0:T(8,128)} %param.9) | non-fusion elementwise | flops 64 | bytes 512 | tf_op jit(solution)/shard_map/convert_element_type | solution.py:521
  2.3 0.0 copy-start
  2.3 106.1 %stacked.1 = f32[8,256]{1,0:T(8,128)} custom-call(f32[8,8]{1,0:T(8,128)} %convert_element_type.14.mask_ref, f32[8,64,128]{2,1,0:T(8,128)} %broadcast_in_dim.2.waves_ref, f32[16,128,1]{2,1,0:T(8,128)} %constant.103.clone.taper_ref, f32[256,4096]{1,0:T(8,128)} %raw_hbm.1, bf16[4,8,512,256]{3,2,1,0:T(8,128)(2,1)} %constant.104.clone.table_hbm, ...), custom_call_target="tpu_custom_call" | custom-call | flops 6442450944 | bytes 26214400 | tf_op jit(solution)/shard_map/stacked/pallas_call | solution.py:482
  108.4 0.0 copy-done
  108.4 0.1 select_reduce_fusion
  108.5 0.1 multiply_reduce_fusion
  108.6 1.3 %broadcast_multiply_fusion = f32[8,256]{1,0:T(8,128)} fusion(f32[8,256]{1,0:T(8,128)} %stacked.1, f32[256]{0:T(256)S(1)} %multiply_rsqrt_fusion), kind=kLoop, calls=%fused_computation.3 | loop fusion | flops 2048 | bytes 17408 | tf_op jit(solution)/shard_map/mul | solution.py:559
  (8 shorter events, 0.1 us)
Async XLA Ops:
  2.3 106.2 %copy-start = (s32[8,8]{1,0:T(8,128)S(1)}, s32[8,8]{1,0:T(8,128)}, u32[]{:S(2)}) copy-start(s32[8,8]{1,0:T(8,128)} %param.9) | copy-start | bytes 772

commit v4 on v3

--- a/solution.py
+++ b/solution.py
@@ -91,6 +91,19 @@
     both[:, :, 0] = 0.0
     both = both.reshape(2, size // chunk, chunk, size).transpose(1, 0, 2, 3)
     return split_high_low(both.reshape(size // chunk, 2 * chunk, size))
+
+
+@functools.cache
+def lag_waves(n_dev):
+    groups = n_dev // RADIX
+    bins = NB // n_dev
+    device = np.arange(n_dev)[:, None]
+    k = RADIX * ((device % groups) * bins + np.arange(bins)[None, :] + 1) + device // groups
+    number = np.arange(LAGS // 2) + LAGS // 2
+    shifts = LAG_STEP * (2 * number + 1 - LAGS) // 2
+    phase = 2 * np.pi * ((shifts[None, :, None] * k[:, None, :]) % NT) / NT
+    waves = np.concatenate([np.cos(phase), np.sin(phase)], axis=1).astype(np.float32)
+    return np.ascontiguousarray(np.broadcast_to(waves[..., None], (*waves.shape, LANES)))
 
 
 def real_dft16(x):
@@ -171,9 +184,51 @@
     @pl.loop(1, n_dev)
     def _(ahead):
         other = (me + ahead) % n_dev
-        copy = slot_copy(src_ref, dst_ref, chunk, other, other, send_sem, recv_sem, other)
-        copy.wait_send()
-        copy.wait_recv()
+        slot_copy(src_ref, dst_ref, chunk, other, other, send_sem, recv_sem, other).wait_recv()
+
+
+def wait_sent(n_dev, chunk, src_ref, dst_ref, send_sem, recv_sem):
+    me = own_index()
+
+    @pl.loop(1, n_dev)
+    def _(ahead):
+        other = (me + ahead) % n_dev
+        slot_copy(src_ref, dst_ref, chunk, other, other, send_sem, recv_sem, other).wait_send()
+
+
+def sum_along(axis, src_ref, got_ref, send_sem, recv_sem, meanwhile):
+    size = lax.axis_size(axis)
+    me = lax.axis_index(axis)
+
+    def copy(src, dst, device):
+        return pltpu.make_async_remote_copy(
+            src_ref=src_ref.at[src],
+            dst_ref=got_ref.at[dst],
+            send_sem=send_sem.at[src],
+            recv_sem=recv_sem.at[dst],
+            device_id={axis: device},
+            device_id_type=pl.DeviceIdType.MESH,
+        )
+
+    @pl.loop(1, size)
+    def _(ahead):
+        other = (me + ahead) % size
+        copy(other, me, other).start()
+
+    got_ref[me] = src_ref[me]
+    meanwhile()
+
+    @pl.loop(1, size)
+    def _(ahead):
+        other = (me + ahead) % size
+        copy(other, other, other).wait_recv()
+
+    @pl.loop(1, size)
+    def _(ahead):
+        other = (me + ahead) % size
+        copy(other, other, other).wait_send()
+
+    return jnp.sum(got_ref[...], axis=0)
 
 
 def transform(series_ref, chunk, y_ref, spec_ref, table_ref):
@@ -249,7 +304,7 @@
             g_re = jnp.zeros((8, chunk), f32)
             g_im = jnp.zeros((8, chunk), f32)
             for block in range(blocks - delta):
-                keep = mask_ref[block, block + delta]
+                keep = mask_ref[block, block + delta].astype(f32)
                 a_re, a_im = re_ref[block, rows, :], im_ref[block, rows, :]
                 if delta == 0:
                     g_re = g_re + keep * (a_re * a_re + a_im * a_im)
@@ -299,8 +354,8 @@
 def stack_kernel(
     blocks,
     mask_ref,
-    waves_ref,
     taper_ref,
+    waves_hbm,
     raw_hbm,
     table_hbm,
     high_hbm,
@@ -308,6 +363,7 @@
     back_high_hbm,
     back_low_hbm,
     out_ref,
+    waves_ref,
     raw_ref,
     table_ref,
     high_ref,
@@ -331,6 +387,8 @@
     acc_ref,
     part_ref,
     got_ref,
+    plane_ref,
+    plane_got_ref,
     raw_sem,
     table_sem,
     raw_send,
@@ -339,6 +397,8 @@
     white_recv,
     stack_send,
     stack_recv,
+    plane_send,
+    plane_recv,
 ):
     _, n_dev, rows, chans = series_ref.shape
     groups = n_dev // RADIX
@@ -356,11 +416,12 @@
             (low_hbm, low_ref),
             (back_high_hbm, back_high_ref),
             (back_low_hbm, back_low_ref),
+            (waves_hbm.at[me], waves_ref),
         )
         src, dst = pairs[n]
         return pltpu.make_async_copy(src, dst, table_sem.at[n])
 
-    n_tables = 5
+    n_tables = 6
 
     for chunk in range(RAW_CHUNKS):
         raw_copy(chunk).start()
@@ -420,6 +481,10 @@
     def _(w):
         start_all(n_dev, w, ready_ref, white_ref, white_send, white_recv)
 
+    @pl.loop(0, RAW_CHUNKS)
+    def _(chunk):
+        wait_sent(n_dev, chunk, cast_ref, series_ref, raw_send, raw_recv)
+
     for n in range(1, n_tables):
         table_copy(n).wait()
     per_block = n_dev // blocks
@@ -447,7 +512,7 @@
         to_offsets(blocks, q, sums_ref, h_ref, back_high_ref, back_low_ref, acc_ref)
 
     width = per_block * chans
-    cols = part_ref.shape[3]
+    n_blk, n_lag, _, cols = part_ref.shape
     parts = width // cols
     for segment in range(2 * blocks):
         value = jnp.zeros((LAGS, width), f32)
@@ -456,14 +521,18 @@
         if segment > 0:
             value = value + acc_ref[pl.ds((segment - 1) * LAGS, LAGS), pl.ds(width, width)]
         for part in range(parts):
-            part_ref[0, segment * parts + part] = value[:, part * cols : (part + 1) * cols]
-    start_all(n_dev, 0, part_ref, got_ref, stack_send, stack_recv)
-    got_ref[0, me] = part_ref[0, me]
-    wait_all(n_dev, 0, part_ref, got_ref, stack_send, stack_recv)
-    out_ref[...] = jnp.sum(got_ref[0], axis=0)
-
-
-def stacked(raw, mask, waves, n_dev):
+            part_ref[*divmod(segment * parts + part, n_lag)] = value[:, part * cols : (part + 1) * cols]
+
+    def finish_white():
+        @pl.loop(0, bin_chunks)
+        def _(w):
+            wait_sent(n_dev, w, ready_ref, white_ref, white_send, white_recv)
+
+    plane_ref[...] = sum_along("blk", part_ref, got_ref, stack_send, stack_recv, finish_white)
+    out_ref[...] = sum_along("lag", plane_ref, plane_got_ref, plane_send, plane_recv, lambda: None)
+
+
+def stacked(raw, mask, n_dev):
     samples = raw.shape[0]
     chans = C // n_dev
     blocks = mask.shape[0]
@@ -472,6 +541,8 @@
     size = 2 * width
     chunk = LANES
     cols = 2 * C // n_dev
+    n_blk, n_lag = lax.axis_size("blk"), lax.axis_size("lag")
+    waves = lag_waves(n_dev)
     bin_chunks = bins // BIN_CHUNK
     pairs = RADIX // 2
     f32, b16 = jnp.float32, jnp.bfloat16
@@ -482,9 +553,10 @@
     return pl.pallas_call(
         functools.partial(stack_kernel, blocks),
         out_shape=jax.ShapeDtypeStruct((LAGS, cols), f32),
-        in_specs=[pl.BlockSpec(memory_space=pltpu.SMEM), whole, whole] + [away] * 6,
+        in_specs=[pl.BlockSpec(memory_space=pltpu.SMEM), whole] + [away] * 7,
         out_specs=whole,
         scratch_shapes=[
+            pltpu.VMEM(waves.shape[1:], f32),
             pltpu.VMEM(raw.shape, f32),
             *[pltpu.VMEM(table.shape, b16) for table in tables],
             pltpu.VMEM((RAW_CHUNKS, n_dev, samples // RAW_CHUNKS, chans), b16),
@@ -502,33 +574,27 @@
             pltpu.VMEM((size // chunk, blocks * 2 * LAGS, 8, chunk), f32),
             pltpu.VMEM((rows, 2 * chunk), f32),
             pltpu.VMEM((rows, size), f32),
-            pltpu.VMEM((1, n_dev, LAGS, cols), f32),
-            pltpu.VMEM((1, n_dev, LAGS, cols), f32),
+            pltpu.VMEM((n_blk, n_lag, LAGS, cols), f32),
+            pltpu.VMEM((n_blk, n_lag, LAGS, cols), f32),
+            pltpu.VMEM((n_lag, LAGS, cols), f32),
+            pltpu.VMEM((n_lag, LAGS, cols), f32),
             pltpu.SemaphoreType.DMA((RAW_CHUNKS,)),
-            pltpu.SemaphoreType.DMA((len(tables),)),
+            pltpu.SemaphoreType.DMA((len(tables) + 1,)),
             pltpu.SemaphoreType.DMA((RAW_CHUNKS, n_dev)),
             pltpu.SemaphoreType.DMA((RAW_CHUNKS, n_dev)),
             pltpu.SemaphoreType.DMA((bin_chunks, n_dev)),
             pltpu.SemaphoreType.DMA((bin_chunks, n_dev)),
-            pltpu.SemaphoreType.DMA((1, n_dev)),
-            pltpu.SemaphoreType.DMA((1, n_dev)),
+            pltpu.SemaphoreType.DMA((n_blk,)),
+            pltpu.SemaphoreType.DMA((n_blk,)),
+            pltpu.SemaphoreType.DMA((n_lag,)),
+            pltpu.SemaphoreType.DMA((n_lag,)),
         ],
         compiler_params=pltpu.CompilerParams(
             vmem_limit_bytes=58 * 2**20, collective_id=0, has_side_effects=True
         ),
         cost_estimate=pl.CostEstimate(flops=6 * 2**30, bytes_accessed=25 * 2**20, transcendentals=0),
         name="stacked",
-    )(mask.astype(f32), waves, jnp.asarray(taper_table()), raw, *[jnp.asarray(table) for table in tables])
-
-
-def lag_waves(device, bins, groups):
-    rho, group = device // groups, device % groups
-    k = RADIX * (group * bins + lax.iota(jnp.int32, bins) + 1) + rho
-    number = lax.iota(jnp.int32, LAGS // 2) + LAGS // 2
-    shifts = LAG_STEP * (2 * number + 1 - LAGS) // 2
-    phase = jnp.mod(shifts[:, None] * k[None, :], NT).astype(jnp.float32) * (2 * math.pi / NT)
-    waves = jnp.concatenate([jnp.cos(phase), jnp.sin(phase)], axis=0)
-    return jnp.broadcast_to(waves[:, :, None], (LAGS, bins, LANES))
+    )(mask, jnp.asarray(taper_table()), jnp.asarray(waves), raw, *[jnp.asarray(table) for table in tables])
 
 
 def pair_counts(mask, columns):
@@ -552,8 +618,7 @@
 def on_device(raw, mask):
     n_dev = lax.axis_size("blk") * lax.axis_size("lag")
     device = own_index()
-    waves = lag_waves(device, NB // n_dev, n_dev // RADIX)
-    total = stacked(raw, mask, waves, n_dev)
+    total = stacked(raw, mask, n_dev)
     n_cols = total.shape[1]
     counts = pair_counts(mask, device * n_cols + lax.iota(jnp.int32, n_cols))
     return total * stack_scale(counts)[None, :]

time: 110 us -> 109 us (level)
    convert_element_type x1 -> x0, other arithmetic: 1.28 us -> none  [stacked(): mask.astype(f32)]
where the time goes in v4:
time: 109 us
  Pallas kernels  107 us (98%)
  other arithmetic  2.2 us (2%)
    pallas_call x1, Pallas kernels, stacked(): pl.pallas_call(functools.partial(stack_kernel, blocks), out_shape=jax.Sha...  107 us

profile of v4, /device:TPU:0, one launch (start us, length us, event | category | flops | bytes accessed | tf_op | source)
XLA Modules:
  0.0 108.9 jit_solution(8448940639428645706)
XLA Ops:
  0.0 0.8 select_reduce_fusion
  0.8 0.1 multiply_reduce_fusion
  0.9 106.7 %stacked.1 = f32[8,256]{1,0:T(8,128)} custom-call(s32[8,8]{1,0:T(8,128)} %mask_ref.1, f32[16,128,1]{2,1,0:T(8,128)} %constant.45.clone.taper_ref, f32[32,8,64,128]{3,2,1,0:T(8,128)} %constant.46.clone.waves_hbm, f32[256,4096]{1,0:T(8,128)} %raw_hbm.1, bf16[4,8,512,256]{3,2,1,0:T(8,128)(2,1)} %constant.47.clone.table_hbm, ...), custom_call_target="tpu_custom_call" | custom-call | flops 6442450944 | bytes 26214400 | tf_op jit(solution)/shard_map/stacked/pallas_call | solution.py:553
  107.6 1.3 %broadcast_multiply_fusion = f32[8,256]{1,0:T(8,128)} fusion(f32[8,256]{1,0:T(8,128)} %stacked.1, f32[256]{0:T(256)S(1)} %multiply_rsqrt_fusion), kind=kLoop, calls=%fused_computation.2 | loop fusion | flops 2048 | bytes 17408 | tf_op jit(solution)/shard_map/mul | solution.py:624
  (5 shorter events, 0.0 us)

commit v5 on v4

--- a/solution.py
+++ b/solution.py
@@ -196,7 +196,7 @@
         slot_copy(src_ref, dst_ref, chunk, other, other, send_sem, recv_sem, other).wait_send()
 
 
-def sum_along(axis, src_ref, got_ref, send_sem, recv_sem, meanwhile):
+def sum_along(axis, src_ref, got_ref, send_sem, recv_sem):
     size = lax.axis_size(axis)
     me = lax.axis_index(axis)
 
@@ -216,7 +216,6 @@
         copy(other, me, other).start()
 
     got_ref[me] = src_ref[me]
-    meanwhile()
 
     @pl.loop(1, size)
     def _(ahead):
@@ -344,11 +343,9 @@
             h_ref[pl.ds(behind, LAGS), pl.ds(0, chunk)] = jnp.concatenate(h_re[::-1], axis=0)
             h_ref[pl.ds(behind, LAGS), pl.ds(chunk, chunk)] = -jnp.concatenate(h_im[::-1], axis=0)
     h_high, h_low = split_rounded(h_ref[...])
-    acc_ref[...] += (
-        jnp.dot(h_high, back_high_ref[q], preferred_element_type=f32)
-        + jnp.dot(h_low, back_high_ref[q], preferred_element_type=f32)
-        + jnp.dot(h_high, back_low_ref[q], preferred_element_type=f32)
-    )
+    count = h_ref.shape[0]
+    both = jnp.dot(jnp.concatenate([h_high, h_low], axis=0), back_high_ref[q], preferred_element_type=f32)
+    acc_ref[...] += both[:count] + both[count:] + jnp.dot(h_high, back_low_ref[q], preferred_element_type=f32)
 
 
 def stack_kernel(
@@ -437,21 +434,30 @@
     meet_all(n_dev)
     start_all(n_dev, 0, cast_ref, series_ref, raw_send, raw_recv)
 
-    @pl.loop(1, RAW_CHUNKS)
+    send_raw(1)
+    start_all(n_dev, 1, cast_ref, series_ref, raw_send, raw_recv)
+
+    @pl.loop(2, RAW_CHUNKS)
     def _(chunk):
         send_raw(chunk)
-        start_all(n_dev, chunk, cast_ref, series_ref, raw_send, raw_recv)
 
     for n in range(n_tables):
         table_copy(n).start()
     spec_ref[...] = jnp.zeros_like(spec_ref)
     sums_ref[...] = jnp.zeros_like(sums_ref)
     acc_ref[...] = jnp.zeros_like(acc_ref)
+    h_ref[...] = jnp.zeros_like(h_ref)
     table_copy(0).wait()
 
     @pl.loop(0, RAW_CHUNKS)
     def _(chunk):
         series_ref[chunk, me] = cast_ref[chunk, me]
+        wait_sent(n_dev, chunk, cast_ref, series_ref, raw_send, raw_recv)
+
+        @pl.when(chunk + 2 < RAW_CHUNKS)
+        def _():
+            start_all(n_dev, chunk + 2, cast_ref, series_ref, raw_send, raw_recv)
+
         wait_all(n_dev, chunk, cast_ref, series_ref, raw_send, raw_recv)
         transform(series_ref, chunk, y_ref, spec_ref, table_ref)
 
@@ -463,7 +469,7 @@
     def _(i):
         rho = (me // groups + 1 + i) % RADIX
         total = all_ref[...] + suf_ref[rho, pl.ds(PAD - 2, M_ROWS), :] + pre_ref[rho, pl.ds(PAD + 2, M_ROWS), :]
-        scale = taper_ref[rho] / (total / (2 * SW + 1) + EPS)
+        scale = taper_ref[rho] / (total * (1.0 / (2 * SW + 1)) + EPS)
         for part in range(2):
             value = (spec_ref[rho, pl.ds(part * M_ROWS, M_ROWS), :] * scale).astype(jnp.bfloat16)
             for g in range(groups):
@@ -477,13 +483,8 @@
             def _():
                 slot_copy(ready_ref, white_ref, 0, other, me, white_send, white_recv, other).start()
 
-    @pl.loop(1, bin_chunks)
-    def _(w):
-        start_all(n_dev, w, ready_ref, white_ref, white_send, white_recv)
-
-    @pl.loop(0, RAW_CHUNKS)
-    def _(chunk):
-        wait_sent(n_dev, chunk, cast_ref, series_ref, raw_send, raw_recv)
+    if bin_chunks > 1:
+        start_all(n_dev, 1, ready_ref, white_ref, white_send, white_recv)
 
     for n in range(1, n_tables):
         table_copy(n).wait()
@@ -493,6 +494,12 @@
     @pl.loop(0, bin_chunks)
     def _(w):
         white_ref[w, me] = ready_ref[w, me]
+        wait_sent(n_dev, w, ready_ref, white_ref, white_send, white_recv)
+
+        @pl.when(w + 2 < bin_chunks)
+        def _():
+            start_all(n_dev, w + 2, ready_ref, white_ref, white_send, white_recv)
+
         wait_all(n_dev, w, ready_ref, white_ref, white_send, white_recv)
         for source in range(n_dev):
             block, place = divmod(source, per_block)
@@ -523,13 +530,10 @@
         for part in range(parts):
             part_ref[*divmod(segment * parts + part, n_lag)] = value[:, part * cols : (part + 1) * cols]
 
-    def finish_white():
-        @pl.loop(0, bin_chunks)
-        def _(w):
-            wait_sent(n_dev, w, ready_ref, white_ref, white_send, white_recv)
-
-    plane_ref[...] = sum_along("blk", part_ref, got_ref, stack_send, stack_recv, finish_white)
-    out_ref[...] = sum_along("lag", plane_ref, plane_got_ref, plane_send, plane_recv, lambda: None)
+    plane_ref[...] = sum_along("blk", part_ref, got_ref, stack_send, stack_recv)
+    total = sum_along("lag", plane_ref, plane_got_ref, plane_send, plane_recv)
+    columns = me * cols + lax.broadcasted_iota(jnp.int32, (LAGS, cols), 1)
+    out_ref[...] = total * stack_scale(pair_counts(mask_ref, blocks, columns))
 
 
 def stacked(raw, mask, n_dev):
@@ -547,7 +551,7 @@
     pairs = RADIX // 2
     f32, b16 = jnp.float32, jnp.bfloat16
     tables = [spectrum_tables(samples), *channel_tables(width, chunk), *offset_tables(width, chunk)]
-    rows = (2 * blocks - 1) * LAGS
+    rows = 2 * blocks * LAGS
     whole = pl.BlockSpec(memory_space=pltpu.VMEM)
     away = pl.BlockSpec(memory_space=pl.ANY)
     return pl.pallas_call(
@@ -597,18 +601,16 @@
     )(mask, jnp.asarray(taper_table()), jnp.asarray(waves), raw, *[jnp.asarray(table) for table in tables])
 
 
-def pair_counts(mask, columns):
-    blocks = mask.shape[0]
+def pair_counts(mask_ref, blocks, columns):
     width = C // blocks
-    labels = lax.iota(jnp.int32, blocks)
-    apart = labels[None, :] - labels[:, None]
-    deltas = lax.iota(jnp.int32, 2 * blocks - 1) - (blocks - 1)
-    per_delta = jnp.sum(
-        mask[None] * (apart[None] == deltas[:, None, None]).astype(jnp.int32), axis=(1, 2)
-    )
     offsets = columns - C
-    intersection = jnp.maximum(0, width - jnp.abs(offsets[:, None] - width * deltas[None, :]))
-    return jnp.sum(intersection * per_delta[None, :], axis=1)
+    counts = jnp.zeros_like(columns)
+    for delta in range(1 - blocks, blocks):
+        per_delta = sum(
+            mask_ref[block, block + delta] for block in range(max(0, -delta), min(blocks, blocks - delta))
+        )
+        counts = counts + jnp.maximum(0, width - jnp.abs(offsets - width * delta)) * per_delta
+    return counts
 
 
 def stack_scale(counts):
@@ -617,11 +619,7 @@
 
 def on_device(raw, mask):
     n_dev = lax.axis_size("blk") * lax.axis_size("lag")
-    device = own_index()
-    total = stacked(raw, mask, n_dev)
-    n_cols = total.shape[1]
-    counts = pair_counts(mask, device * n_cols + lax.iota(jnp.int32, n_cols))
-    return total * stack_scale(counts)[None, :]
+    return stacked(raw, mask, n_dev)
 
 
 def solution(mesh):

time: 109 us -> 108 us (level)
  other arithmetic: 2.2 us -> 0 us
  local copies, waits for them, and re-layouts: 0 us -> 1.3 us
    mul x2 -> x0, other arithmetic: 1.3 us -> none  [the longest x1 1.3 us: on_device(): return total * stack_scale(counts)[None, :]]
    unnamed x0 -> x1, local copies, waits for them, and re-layouts: none -> 1.3 us
where the time goes in v5:
time: 108 us
  Pallas kernels  106 us (98%)
  local copies, waits for them, and re-layouts  1.3 us (1%)
    pallas_call x1, Pallas kernels, stacked(): pl.pallas_call(functools.partial(stack_kernel, blocks), out_shape=jax.Sha...  106 us

profile of v5, /device:TPU:0, one launch (start us, length us, event | category | flops | bytes accessed | tf_op | source)
XLA Modules:
  0.0 107.5 jit_solution(11883933138219189824)
XLA Ops:
  0.0 106.2 %stacked.1 = f32[8,256]{1,0:T(8,128)} custom-call(s32[8,8]{1,0:T(8,128)} %mask_ref.1, f32[16,128,1]{2,1,0:T(8,128)} %constant.14.clone.taper_ref, f32[32,8,64,128]{3,2,1,0:T(8,128)} %constant.15.clone.waves_hbm, f32[256,4096]{1,0:T(8,128)} %raw_hbm.1, bf16[4,8,512,256]{3,2,1,0:T(8,128)(2,1)} %constant.16.clone.table_hbm, ...), custom_call_target="tpu_custom_call" | custom-call | flops 6442450944 | bytes 26214400 | tf_op jit(solution)/shard_map/stacked/pallas_call | solution.py:557
  106.2 1.3 %copy.11 = f32[8,256]{1,0:T(8,128)} copy(f32[8,256]{1,0:T(8,128)} %stacked.1) | data formatting | bytes 16384

commit v6 on v5

--- a/solution.py
+++ b/solution.py
@@ -21,7 +21,7 @@
 EPS = 1e-06
 
 RADIX = 16
-RAW_CHUNKS = 4
+RAW_CHUNKS = 2
 BIN_CHUNK = 16
 SPAN = NT // RADIX
 M_ROWS = NB // RADIX

time: 108 us -> 108 us (level)
  no operation moved by 1% of the time
where the time goes in v6:
time: 108 us
  Pallas kernels  107 us (99%)
  local copies, waits for them, and re-layouts  1.3 us (1%)
    pallas_call x1, Pallas kernels, stacked(): pl.pallas_call(functools.partial(stack_kernel, blocks), out_shape=jax.Sha...  107 us

profile of v6, /device:TPU:0, one launch (start us, length us, event | category | flops | bytes accessed | tf_op | source)
XLA Modules:
  0.0 108.0 jit_solution(14454810931633027910)
XLA Ops:
  0.0 106.7 %stacked.1 = f32[8,256]{1,0:T(8,128)} custom-call(s32[8,8]{1,0:T(8,128)} %mask_ref.1, f32[16,128,1]{2,1,0:T(8,128)} %constant.14.clone.taper_ref, f32[32,8,64,128]{3,2,1,0:T(8,128)} %constant.15.clone.waves_hbm, f32[256,4096]{1,0:T(8,128)} %raw_hbm.1, bf16[2,8,512,512]{3,2,1,0:T(8,128)(2,1)} %constant.16.clone.table_hbm, ...), custom_call_target="tpu_custom_call" | custom-call | flops 6442450944 | bytes 26214400 | tf_op jit(solution)/shard_map/stacked/pallas_call | solution.py:557
  106.7 1.3 %copy.11 = f32[8,256]{1,0:T(8,128)} copy(f32[8,256]{1,0:T(8,128)} %stacked.1) | data formatting | bytes 16384
